TPU v7x, 32 devices: a whole 2x2x4 slice. The times are simulated.
32 devices in a mesh: pair: 8 (over z, y), seg: 4 (over x, core).
Axes of the slice: x: 2, y: 2, z: 4, core: 2. Of those that a mesh axis runs over, the one named last changes fastest.
Arguments:
- traces: bfloat16 [8, 128, 32768], P('pair', None, 'seg'), may hold values from -6 to 6
- pairs: int32 [8, 2], P('pair'), may hold values from 0 to 7
- block_row: int32 [8], replicated, may hold values from 0 to 7, each once
Outputs:
- stack: float32 [8, 128, 2048], P('pair', 'seg')
Inputs may be any that keep to these rules, and one draw needn't show every extreme that they name: `pairs`: each entry is a block number. `block_row`: a permutation of the block numbers.
All inputs are finite; a program needn't handle non-finite values.
Results may differ from a plain program's by a relative error of at most 0.0044.
Values may be sent and summed in bfloat16 or wider, within the bound.
No kernel may reach another device: no remote copies, remote signals or barrier semaphores. Data moves between devices by JAX's collectives and lax.ppermute only.
A program may use at most 64 MiB of HBM per device.

v0:
```python
import jax
import jax.numpy as jnp
from jax import lax
from jax.sharding import PartitionSpec as P

WIN = 2048
NB = 512
LAGS = 2048


def forward_table(bins, width):
    freq = jnp.arange(bins, dtype=jnp.int32) + 1
    times = jnp.arange(width, dtype=jnp.int32)
    phase = (freq[:, None] * times[None, :] % width).astype(jnp.float32) * (2.0 * jnp.pi / width)
    return jnp.stack((jnp.cos(phase), -jnp.sin(phase))).astype(jnp.bfloat16)


def inverse_table(bins, lags, width):
    freq = jnp.arange(bins, dtype=jnp.int32) + 1
    shifts = jnp.arange(lags, dtype=jnp.int32) - lags // 2
    phase = (freq[:, None] * shifts[None, :] % width).astype(jnp.float32) * (2.0 * jnp.pi / width)
    return jnp.stack((jnp.cos(phase), -jnp.sin(phase)))


def cross_spectrum(first, second):
    first_re = first[:, 0].astype(jnp.float32)
    first_im = first[:, 1].astype(jnp.float32)
    second_re = second[:, 0].astype(jnp.float32)
    second_im = second[:, 1].astype(jnp.float32)
    real = jnp.sum(first_re * second_re + first_im * second_im, axis=2)
    imag = jnp.sum(first_re * second_im - first_im * second_re, axis=2)
    return jnp.stack((real, imag), axis=1)


def local(traces, pairs, block_row):
    blocks, channels, samples = traces.shape
    windows = samples // WIN
    table = forward_table(NB, WIN)
    frames = traces.reshape(blocks, channels, windows, WIN)
    spectra = jnp.einsum("skt,bcwt->bskwc", table, frames, preferred_element_type=jnp.float32)
    power = jnp.mean(spectra[:, 0] * spectra[:, 0] + spectra[:, 1] * spectra[:, 1], axis=-1)
    whitened = (spectra / jnp.sqrt(power + 1e-06)[:, None, :, :, None]).astype(jnp.bfloat16)
    all_pairs = lax.all_gather(pairs, "pair", axis=0, tiled=True)
    rows_first = block_row[all_pairs[:, 0]]
    rows_second = block_row[all_pairs[:, 1]]
    by_bin = lax.all_to_all(whitened, "pair", split_axis=2, concat_axis=0, tiled=True)
    first = by_bin[rows_first]
    second = by_bin[rows_second]
    both = jnp.stack((first, second), axis=1)
    mine = lax.all_to_all(both, "pair", split_axis=0, concat_axis=3, tiled=True)
    cross = cross_spectrum(mine[:, 0], mine[:, 1])
    back = inverse_table(NB, LAGS, WIN)
    scale = 1.0 / (windows * lax.axis_size("seg"))
    correlated = jnp.einsum("pskc,skl->pcl", cross, back, precision=lax.Precision.HIGHEST)
    summed = lax.psum_scatter(correlated, "seg", scatter_dimension=1, tiled=True)
    return summed * scale


def solution(mesh):
    placed = (P("pair", None, "seg"), P("pair", None), P())
    return jax.shard_map(
        local, mesh=mesh, in_specs=placed, out_specs=P("pair", "seg", None), check_vma=False
    )
```

profile of v0, /device:TPU:0, one launch (start us, length us, event | category | flops | bytes accessed | tf_op | source)
XLA Modules:
  0.0 187.8 jit_solution(12253957133933507605)
XLA Ops:
  6.5 0.0 copy-start
  6.5 3.3 %reshape.421 = bf16[128,4,2048]{2,1,0:T(4,128)(2,1)S(1)} reshape(bf16[1,128,8192]{2,1,0:T(8,128)(2,1)} %param.3) | data formatting | bytes 4194304 | tf_op jit(solution)/shard_map/reshape
  9.9 35.4 %cosine_convert_fusion = (bf16[1,512,2048]{2,1,0:T(8,128)(2,1)S(1)}, bf16[1,512,2048]{2,1,0:T(8,128)(2,1)S(1)}, f32[1,512,2048]{2,1,0:T(8,128)}, f32[1,512,2048]{2,1,0:T(8,128)}) fusion(s32[512]{0:T(512)S(1)} %iota_add_fusion.1, s32[2048]{0:T(1024)S(1)} %iota_add_fusion), kind=kLoop, calls=%fused_computation.28 | loop fusion | flops 33554432 | bytes 12593152 | tf_op jit(solution)/shard_map/convert
  45.2 3.8 %fusion.22 = f32[1,2,512,4,128]{2,4,3,1,0:T(8,128)S(1)} fusion(bf16[128,4,2048]{2,1,0:T(4,128)(2,1)S(1)} %reshape.421, bf16[1,512,2048]{2,1,0:T(8,128)(2,1)S(1)} %get-tuple-element.12, bf16[1,512,2048]{2,1,0:T(8,128)(2,1)S(1)} %get-tuple-element.11), kind=kOutput, calls=%fused_computation.38 | convolution fusion | flops 2155872256 | bytes 8388608 | tf_op jit(solution)/shard_map/skt,bcwt->bskwc/dot_general | solution.py:40
  49.1 0.3 fusion.30
  49.3 0.0 copy-start.1
  49.3 0.3 divide_convert_fusion
  49.7 1.5 copy.12
  51.2 7.3 %all-to-all-start = ((bf16[1,2,512,4,128]{4,3,1,0,2:T(4,128)(2,1)}), bf16[1,2,512,4,128]{4,3,1,0,2:T(4,128)(2,1)S(1)}, u32[]{:S(2)}, u32[]{:S(2)}) async-start(bf16[1,2,512,4,128]{4,3,1,0,2:T(4,128)(2,1)} %copy.12), calls=%async_computation | async-start | bytes 2097152 | tf_op jit(solution)/shard_map/all_to_all | solution.py:46
  58.5 0.0 reduce-scatter.2.cloned.1.call-start
  58.5 0.0 copy-done.1
  58.5 31.5 %all-gather = s32[8,1,2]{2,1,0:T(1,128)S(1)} all-gather(s32[1,1,2]{2,1,0:T(1,128)S(1)} %bitcast.66), channel_id=1, replica_groups=mesh['pair'=8,'seg'=4] {'pair'}, dimensions={0}, use_global_device_ids=true | all-gather | bytes 72 | tf_op jit(solution)/shard_map/all_gather | solution.py:43
  90.0 0.1 copy.15
  90.1 0.0 copy-done
  90.1 0.6 gather_fusion.2
  90.8 0.6 gather_fusion
  91.5 0.0 all-to-all-done
  91.5 0.3 copy.30
  91.8 0.8 gather_fusion.3
  92.5 0.7 gather_fusion.1
  93.3 0.2 pad_maximum_fusion
  93.5 0.3 copy.16
  93.8 51.1 %all_to_all.36 = bf16[8,2,2,64,4,128]{5,3,4,2,1,0:T(8,128)(2,1)S(1)} all-to-all(bf16[8,2,2,64,4,128]{5,3,4,2,1,0:T(8,128)(2,1)S(1)} %copy.16), channel_id=1, replica_groups=mesh['pair'=8,'seg'=4] {'pair'}, dimensions={0} | all-to-all | bytes 4194304 | tf_op jit(solution)/shard_map/all_to_all | solution.py:50
  144.9 0.2 copy.17
  145.1 0.2 slice_bitcast_fusion.1
  145.3 0.4 fusion.26
  145.8 0.1 copy.19
  145.9 0.1 copy.18
  146.1 9.1 %fusion.16 = f32[1,128,2048]{2,1,0:T(8,128)} fusion(f32[1,512,2048]{2,1,0:T(8,128)} %get-tuple-element.13, f32[1,512,2048]{2,1,0:T(8,128)} %get-tuple-element.14, f32[1,1,512,128]{2,3,1,0:T(8,128)S(1)} %bitcast.63, f32[1,1,512,128]{2,3,1,0:T(8,128)S(1)} %bitcast.64), kind=kOutput, calls=%fused_computation.32 | convolution fusion | flops 3223453696 | bytes 9961472 | tf_op jit(solution)/shard_map/pskc,skl->pcl/dot_general | solution.py:54
  155.1 0.0 reduce-scatter.2.cloned.1.call-update
  155.2 24.1 %reduce-scatter.2.cloned.1.call-done = f32[1,32,2048]{2,1,0:T(8,128)} async-done(((f32[1,128,2048]{2,1,0:T(8,128)}), f32[1,32,2048]{2,1,0:T(8,128)}) %reduce-scatter.2.cloned.1.call-update) | async-done | bytes 262160 | tf_op jit(solution)/shard_map/reduce_scatter | solution.py:55
  179.3 1.7 broadcast_multiply_fusion
  (9 shorter events, 0.1 us)
Async XLA Ops:
  6.5 83.6 %copy-start = (s32[8]{0:T(128)S(1)}, s32[8]{0:T(128)}, u32[]{:S(2)}) copy-start(s32[8]{0:T(128)} %param.5) | copy-start | bytes 100
  49.3 9.2 %copy-start.1 = (s32[1,2]{1,0:T(1,128)S(1)}, s32[1,2]{1,0:T(1,128)}, u32[]{:S(2)}) copy-start(s32[1,2]{1,0:T(1,128)} %param.4) | copy-start | bytes 28
  51.2 40.3 %all-to-all-start = ((bf16[1,2,512,4,128]{4,3,1,0,2:T(4,128)(2,1)}), bf16[1,2,512,4,128]{4,3,1,0,2:T(4,128)(2,1)S(1)}, u32[]{:S(2)}, u32[]{:S(2)}) async-start(bf16[1,2,512,4,128]{4,3,1,0,2:T(4,128)(2,1)} %copy.12), calls=%async_computation | async-start | bytes 2097152 | tf_op jit(solution)/shard_map/all_to_all | solution.py:46
  58.5 120.8 %reduce-scatter.2.cloned.1.call-start = ((), (), s32[]{:S(2)}) async-start(), calls=%async_computation.3 | async-start | bytes 1310720 | tf_op jit(solution)/shard_map/reduce_scatter | solution.py:55
Sparse Core Ops, SparseCore 0:
  155.3 23.9 reduce-scatter.1
where the time goes:
time: 188 us
  blocking collectives  82.6 us (44%)
  other arithmetic  38.3 us (20%)
  waiting for transfers between devices  24.2 us (13%)
  between operations  13.6 us (7%)
  matrix products  12.9 us (7%)
  local copies, waits for them, and re-layouts  8.96 us (5%)
  starting transfers between devices  7.32 us (4%)
    all_to_all x1, blocking collectives, local(): mine = lax.all_to_all(both, 'pair', split_axis=0, concat_axis=3, tiled=True)  51.1 us
    another operation x1, other arithmetic  35.4 us
    all_gather x1, blocking collectives, local(): all_pairs = lax.all_gather(pairs, 'pair', axis=0, tiled=True)  31.5 us
    reduce_scatter x1, waiting for transfers between devices, local(): lax.psum_scatter(correlated, 'seg', scatter_dimension=1, tiled=True)  24.1 us
    dot_general x1, matrix products, local(): jnp.einsum('pskc,skl->pcl', cross, back, precision=lax.Precision.HIGHEST)  9.08 us
    all_to_all x1, starting transfers between devices, local(): lax.all_to_all(whitened, 'pair', split_axis=2, concat_axis=0, tiled=True)  7.28 us
    dot_general x1, matrix products, local(): jnp.einsum('skt,bcwt->bskwc', table, frames, preferred_element_type=jnp.f...  3.81 us
  transfers between devices with their start and end apart: 2, of which 1 were waited for; matrix products, arithmetic and copies ran while one was open for 1% of the time, Pallas kernels for 0%

commit v1 on v0

v1 whole, which is shorter than its diff:
```python
import functools

import jax
import jax.numpy as jnp
import ml_dtypes
import numpy as np
from jax import lax
from jax.experimental import pallas as pl
from jax.experimental.pallas import tpu as pltpu
from jax.sharding import PartitionSpec as P

WIN = 2048
NB = 512
LAGS = 2048
HALF = WIN // 2
LANES = 128
BINS = LANES // 2
TILES = NB // BINS
GROUP = 2


def frequencies():
    even = np.arange(2, NB + 1, 2)
    odd = np.arange(1, NB + 1, 2)
    return np.concatenate((even, odd)).reshape(TILES, BINS)


def forward_table():
    phase = (frequencies()[:, :, None] * np.arange(HALF) % WIN) * (2.0 * np.pi / WIN)
    table = np.stack((np.cos(phase), -np.sin(phase)), axis=1)
    return table.reshape(TILES * LANES, HALF).T.astype(ml_dtypes.bfloat16)


def inverse_table(scale):
    shifts = np.arange(LAGS // 2) - LAGS // 2
    phase = (frequencies()[:, :, None] * shifts % WIN) * (2.0 * np.pi / WIN)
    table = np.stack((np.cos(phase), -np.sin(phase)), axis=1) * scale
    return table.reshape(TILES * LANES, LAGS // 2).astype(ml_dtypes.bfloat16)


def whiten_kernel(windows, segs, traces_ref, table_ref, out_ref):
    channels = traces_ref.shape[0]
    halves = [traces_ref[:, k * HALF : (k + 1) * HALF] for k in range(2 * windows)]
    product = jnp.dot(
        jnp.concatenate(halves, axis=0), table_ref[...], preferred_element_type=jnp.float32
    )
    sign = jnp.where(pl.program_id(0) * GROUP < TILES // 2, 1.0, -1.0)
    for w in range(windows):
        first = product[2 * w * channels : (2 * w + 1) * channels]
        second = product[(2 * w + 1) * channels : (2 * w + 2) * channels]
        spectra = first + sign * second
        power = jnp.sum(spectra * spectra, axis=0, keepdims=True) * (1.0 / channels)
        for tile in range(GROUP):
            cols = slice(tile * LANES, (tile + 1) * LANES)
            both = power[:, cols]
            both = both + pltpu.roll(both, BINS, 1)
            white = spectra[:, cols] * lax.rsqrt(both + 1e-06)
            out_ref[tile, :, w] = white.astype(jnp.bfloat16).reshape(segs, channels // segs, LANES)


def whiten(traces, windows, segs):
    channels, samples = traces.shape
    shape = (TILES, segs, windows, channels // segs, LANES)
    return pl.pallas_call(
        functools.partial(whiten_kernel, windows, segs),
        grid=(TILES // GROUP,),
        in_specs=[
            pl.BlockSpec((channels, samples), lambda i: (0, 0)),
            pl.BlockSpec((HALF, GROUP * LANES), lambda i: (0, i)),
        ],
        out_specs=pl.BlockSpec((GROUP,) + shape[1:], lambda i: (i, 0, 0, 0, 0)),
        out_shape=jax.ShapeDtypeStruct(shape, jnp.bfloat16),
        compiler_params=pltpu.CompilerParams(vmem_limit_bytes=24 * 2**20),
        name="whiten",
    )(traces, jnp.asarray(forward_table()))


def cross_kernel(pairs_ref, row_ref, spectra_ref, out_ref):
    count, channels, lanes = out_ref.shape
    frames = spectra_ref.shape[1]
    low = lax.broadcasted_iota(jnp.int32, (channels, lanes), 1) < lanes // 2

    def one(i, carry):
        a = row_ref[pairs_ref[i, 0]]
        b = row_ref[pairs_ref[i, 1]]
        straight = jnp.zeros((channels, lanes), jnp.float32)
        crossed = jnp.zeros((channels, lanes), jnp.float32)
        for w in range(frames):
            first = spectra_ref[a, w].astype(jnp.float32)
            second = spectra_ref[b, w].astype(jnp.float32)
            straight += first * second
            crossed += first * pltpu.roll(second, lanes // 2, 1)
        real = straight + pltpu.roll(straight, lanes // 2, 1)
        imag = pltpu.roll(crossed, lanes // 2, 1) - crossed
        out_ref[i] = jnp.where(low, real, imag).astype(jnp.bfloat16)
        return carry

    lax.fori_loop(0, count, one, 0)


def cross_tiles(pairs, block_row, spectra):
    rows, frames, channels, lanes = spectra.shape
    smem = pl.BlockSpec(memory_space=pltpu.SMEM)
    vmem = pl.BlockSpec(memory_space=pltpu.VMEM)
    return pl.pallas_call(
        cross_kernel,
        in_specs=[smem, smem, vmem],
        out_specs=vmem,
        out_shape=jax.ShapeDtypeStruct((pairs.shape[0], channels, lanes), jnp.bfloat16),
        compiler_params=pltpu.CompilerParams(vmem_limit_bytes=8 * 2**20),
        name="cross",
    )(pairs, block_row, spectra)


def cross_bands(pairs, block_row, spectra):
    rows, frames, channels, lanes = spectra.shape
    parts = spectra.reshape(rows, frames, channels, 2, lanes // 2)
    first = parts[block_row[pairs[:, 0]]].astype(jnp.float32)
    second = parts[block_row[pairs[:, 1]]].astype(jnp.float32)
    real = jnp.sum(first[:, :, :, 0] * second[:, :, :, 0] + first[:, :, :, 1] * second[:, :, :, 1], axis=1)
    imag = jnp.sum(first[:, :, :, 0] * second[:, :, :, 1] - first[:, :, :, 1] * second[:, :, :, 0], axis=1)
    return jnp.concatenate((real, imag), axis=2).astype(jnp.bfloat16)


def inverse_kernel(cross_ref, table_ref, out_ref):
    half = TILES // 2
    even = jnp.concatenate([cross_ref[k] for k in range(half)], axis=1)
    odd = jnp.concatenate([cross_ref[k] for k in range(half, TILES)], axis=1)
    depth = half * LANES
    a = jnp.dot(even, table_ref[:depth], preferred_element_type=jnp.float32)
    b = jnp.dot(odd, table_ref[depth:], preferred_element_type=jnp.float32)
    out_ref[0, :, : LAGS // 2] = a + b
    out_ref[0, :, LAGS // 2 :] = a - b


def inverse(cross, scale):
    vmem = pl.BlockSpec(memory_space=pltpu.VMEM)
    return pl.pallas_call(
        inverse_kernel,
        in_specs=[vmem, vmem],
        out_specs=vmem,
        out_shape=jax.ShapeDtypeStruct((1, cross.shape[1], LAGS), jnp.float32),
        compiler_params=pltpu.CompilerParams(vmem_limit_bytes=16 * 2**20),
        name="inverse",
    )(cross, jnp.asarray(inverse_table(scale)))


def local(traces, pairs, block_row):
    _, channels, samples = traces.shape
    windows = samples // WIN
    bands, segs = lax.axis_size("pair"), lax.axis_size("seg")
    per_tile = bands // TILES
    share = channels // segs
    width = 2 * NB // bands
    all_pairs = lax.all_gather(pairs, "pair", axis=0, tiled=True)
    white = whiten(traces[0], windows, segs)
    if per_tile > 1:
        white = white.reshape(TILES, segs, windows, share, 2, per_tile, width // 2)
        white = white.transpose(0, 5, 1, 2, 3, 4, 6)
    sent = white.reshape(bands * segs, windows, share, width)
    held = lax.all_to_all(sent, ("pair", "seg"), split_axis=0, concat_axis=0, tiled=True)
    held = held.reshape(bands, segs * windows, share, width)
    cross_of = cross_tiles if width == LANES else cross_bands
    cross = cross_of(all_pairs, block_row, held)
    mine = lax.all_to_all(cross, "pair", split_axis=0, concat_axis=0, tiled=True)
    if per_tile > 1:
        mine = mine.reshape(TILES, per_tile, share, 2, width // 2).transpose(0, 2, 3, 1, 4)
        mine = mine.reshape(TILES, share, LANES)
    return inverse(mine, 1.0 / (windows * segs))


def solution(mesh):
    placed = (P("pair", None, "seg"), P("pair", None), P())
    return jax.shard_map(
        local, mesh=mesh, in_specs=placed, out_specs=P("pair", "seg", None), check_vma=False
    )
```

time: 188 us -> 62.8 us (0.33)
  other arithmetic: 38.3 us -> 0 us
  blocking collectives: 82.6 us -> 44.6 us
  waiting for transfers between devices: 24.2 us -> 0.01 us
  between operations: 13.6 us -> 0.02 us
  matrix products: 12.9 us -> 0 us
  Pallas kernels: 0 us -> 7.46 us
  local copies, waits for them, and re-layouts: 8.96 us -> 3.19 us
    all_to_all x1, blocking collectives: 51.1 us -> 12.6 us  [local(): lax.all_to_all(cross, 'pair', split_axis=0, concat_axis=0, tiled=True)]
    another operation x2 -> x0, other arithmetic: 35.6 us -> none
    reduce_scatter x1 -> x0, waiting for transfers between devices: 24.1 us -> none  [local(): lax.psum_scatter(correlated, 'seg', scatter_dimension=1, tiled=True)]
    dot_general x2 -> x0, matrix products: 12.9 us -> none  [the longest x1 9.08 us: local(): jnp.einsum('pskc,skl->pcl', cross, back, precision=lax.Precision.HIGHEST)]
    pallas_call x0 -> x3, Pallas kernels: none -> 7.46 us  [the longest x1 4.25 us: whiten(): pl.pallas_call(functools.partial(whiten_kernel, windows, segs), grid=(TIL...]
    reshape x1 -> x0, local copies, waits for them, and re-layouts: 3.32 us -> none
    unnamed x4 -> x10, local copies, waits for them, and re-layouts: 0.01 us -> 3.19 us
    gather x4 -> x0, local copies, waits for them, and re-layouts: 2.8 us -> none  [the longest x1 0.76 us: local(): second = by_bin[rows_second]]
  transfers between devices with their start and end apart: 2 -> 1, of which waited for: 1 -> 0; matrix products, arithmetic and copies ran while one was open for 1% -> 0% of each run, Pallas kernels for 0% -> 0%
where the time goes in v1:
time: 62.8 us; the launch traced here: 62.6 us
  blocking collectives  44.6 us (71%)
  Pallas kernels  7.46 us (12%)
  starting transfers between devices  7.29 us (12%)
  local copies, waits for them, and re-layouts  3.19 us (5%)
    all_gather x1, blocking collectives, local(): all_pairs = lax.all_gather(pairs, 'pair', axis=0, tiled=True)  32.1 us
    all_to_all x1, blocking collectives, local(): lax.all_to_all(cross, 'pair', split_axis=0, concat_axis=0, tiled=True)  12.6 us
    all_to_all x1, starting transfers between devices, local(): lax.all_to_all(sent, ('pair', 'seg'), split_axis=0, concat_axis=0, tiled=...  7.29 us
    pallas_call x1, Pallas kernels, whiten(): pl.pallas_call(functools.partial(whiten_kernel, windows, segs), grid=(TIL...  4.25 us
    unnamed x10, local copies, waits for them, and re-layouts  3.19 us
    pallas_call x1, Pallas kernels, cross_tiles(): pl.pallas_call(cross_kernel, in_specs=[smem, smem, vmem], out_specs=vmem,...  2.03 us
  transfers between devices with their start and end apart: 1, of which 0 were waited for; matrix products, arithmetic and copies ran while one was open for 0% of the time, Pallas kernels for 0%

profile of v1, /device:TPU:0, one launch (start us, length us, event | category | flops | bytes accessed | tf_op | source)
XLA Modules:
  0.0 62.6 jit_solution(7245267419364701754)
XLA Ops:
  0.0 0.0 copy-start.1
  0.0 1.6 %copy-done.1 = bf16[1,128,8192]{2,1,0:T(8,128)(2,1)S(1)} copy-done((bf16[1,128,8192]{2,1,0:T(8,128)(2,1)S(1)}, bf16[1,128,8192]{2,1,0:T(8,128)(2,1)}, u32[]{:S(2)}) %copy-start.1) | copy-done | bytes 2097176
  1.6 0.0 copy-start.2
  1.6 1.6 %copy-done.2 = bf16[1024,1024]{1,0:T(8,128)(2,1)S(1)} copy-done((bf16[1024,1024]{1,0:T(8,128)(2,1)S(1)}, bf16[1024,1024]{1,0:T(8,128)(2,1)}, u32[]{:S(2)}) %copy-start.2) | copy-done | bytes 2097176
  3.2 4.2 %whiten.1 = bf16[8,4,4,32,128]{4,3,2,1,0:T(8,128)(2,1)} custom-call(bf16[128,8192]{1,0:T(8,128)(2,1)S(1)} %bitcast.6, bf16[1024,1024]{1,0:T(8,128)(2,1)S(1)} %copy-done.2), custom_call_target="tpu_custom_call" | custom-call | tf_op jit(solution)/shard_map/whiten/pallas_call | solution.py:64
  7.4 0.0 copy-start.4
  7.4 0.0 copy-start.3
  7.4 0.0 copy-start
  7.4 7.3 %all-to-all-start = ((bf16[32,4,32,128]{3,2,1,0:T(8,128)(2,1)}), bf16[32,4,32,128]{3,2,1,0:T(8,128)(2,1)S(1)}, u32[]{:S(2)}, u32[]{:S(2)}) async-start(bf16[32,4,32,128]{3,2,1,0:T(8,128)(2,1)} %bitcast.3), calls=%async_computation | async-start | bytes 2097152 | tf_op jit(solution)/shard_map/all_to_all | solution.py:161
  14.7 0.0 copy-done.4
  14.7 32.1 %all-gather = s32[8,1,2]{2,1,0:T(1,128)S(1)} all-gather(s32[1,1,2]{2,1,0:T(1,128)S(1)} %bitcast.8), channel_id=1, replica_groups=mesh['pair'=8,'seg'=4] {'pair'}, dimensions={0}, use_global_device_ids=true | all-gather | bytes 72 | tf_op jit(solution)/shard_map/all_gather | solution.py:155
  46.8 0.0 all-to-all-done
  46.8 0.0 copy-done.3
  46.8 2.0 %cross.1 = bf16[8,32,128]{2,1,0:T(8,128)(2,1)S(1)} custom-call(s32[8,2]{1,0:T(8,128)S(1)} %bitcast.7, s32[8]{0:T(128)S(1)} %copy-done.3, bf16[8,16,32,128]{3,2,1,0:T(8,128)(2,1)S(1)} %bitcast.5), custom_call_target="tpu_custom_call" | custom-call | tf_op jit(solution)/shard_map/cross/pallas_call | solution.py:105
  48.8 12.6 %all_to_all.10.cross_ref = bf16[8,32,128]{2,1,0:T(8,128)(2,1)S(1)} all-to-all(bf16[8,32,128]{2,1,0:T(8,128)(2,1)S(1)} %cross.1), channel_id=1, replica_groups=mesh['pair'=8,'seg'=4] {'pair'}, dimensions={0} | all-to-all | bytes 131072 | tf_op jit(solution)/shard_map/all_to_all | solution.py:165
  61.4 0.0 copy-done
  61.4 1.2 %inverse.1 = f32[1,32,2048]{2,1,0:T(8,128)} custom-call(bf16[8,32,128]{2,1,0:T(8,128)(2,1)S(1)} %all_to_all.10.cross_ref, bf16[1024,1024]{1,0:T(8,128)(2,1)S(1)} %copy-done), custom_call_target="tpu_custom_call" | custom-call | tf_op jit(solution)/shard_map/inverse/pallas_call | solution.py:138
Async XLA Ops:
  0.0 1.6 %copy-start.1 = (bf16[1,128,8192]{2,1,0:T(8,128)(2,1)S(1)}, bf16[1,128,8192]{2,1,0:T(8,128)(2,1)}, u32[]{:S(2)}) copy-start(bf16[1,128,8192]{2,1,0:T(8,128)(2,1)} %param.5) | copy-start | bytes 6291460
  1.6 1.6 %copy-start.2 = (bf16[1024,1024]{1,0:T(8,128)(2,1)S(1)}, bf16[1024,1024]{1,0:T(8,128)(2,1)}, u32[]{:S(2)}) copy-start(bf16[1024,1024]{1,0:T(8,128)(2,1)} %constant.4.clone.table_ref) | copy-start | bytes 6291460
  7.4 7.3 %copy-start.4 = (s32[1,2]{1,0:T(1,128)S(1)}, s32[1,2]{1,0:T(1,128)}, u32[]{:S(2)}) copy-start(s32[1,2]{1,0:T(1,128)} %param.6) | copy-start | bytes 28
  7.4 39.4 %copy-start.3 = (s32[8]{0:T(128)S(1)}, s32[8]{0:T(128)}, u32[]{:S(2)}) copy-start(s32[8]{0:T(128)} %row_ref.1) | copy-start | bytes 100
  7.4 54.0 %copy-start = (bf16[1024,1024]{1,0:T(8,128)(2,1)S(1)}, bf16[1024,1024]{1,0:T(8,128)(2,1)}, u32[]{:S(2)}) copy-start(bf16[1024,1024]{1,0:T(8,128)(2,1)} %constant.5.clone.table_ref) | copy-start | bytes 6291460
  7.4 39.4 %all-to-all-start = ((bf16[32,4,32,128]{3,2,1,0:T(8,128)(2,1)}), bf16[32,4,32,128]{3,2,1,0:T(8,128)(2,1)S(1)}, u32[]{:S(2)}, u32[]{:S(2)}) async-start(bf16[32,4,32,128]{3,2,1,0:T(8,128)(2,1)} %bitcast.3), calls=%async_computation | async-start | bytes 2097152 | tf_op jit(solution)/shard_map/all_to_all | solution.py:161

commit v2 on v0

v2 whole, which is shorter than its diff:
```python
import functools

import jax
import jax.numpy as jnp
import ml_dtypes
import numpy as np
from jax import lax
from jax.experimental import pallas as pl
from jax.experimental.pallas import tpu as pltpu
from jax.sharding import PartitionSpec as P

WIN = 2048
NB = 512
LAGS = 2048
HALF = WIN // 2
BINS = 128
GROUPS = NB // BINS
SPLIT = 2
PARITIES = 2
NOTE = 8


def frequencies():
    even = np.arange(2, NB + 1, 2)
    odd = np.arange(1, NB + 1, 2)
    return np.concatenate((even, odd)).reshape(GROUPS, BINS)


def forward_table():
    phase = (frequencies()[:, :, None] * np.arange(HALF) % WIN) * (2.0 * np.pi / WIN)
    table = np.stack((np.cos(phase), -np.sin(phase)), axis=1).reshape(PARITIES, NB, HALF)
    return np.ascontiguousarray(table.transpose(0, 2, 1)).astype(ml_dtypes.bfloat16)


def inverse_table(scale):
    shifts = np.arange(LAGS // 2) - LAGS // 2
    phase = (frequencies()[:, :, None] * shifts % WIN) * (2.0 * np.pi / WIN)
    table = np.stack((np.cos(phase), -np.sin(phase)), axis=1) * scale
    return table.reshape(2 * NB, LAGS // 2).astype(ml_dtypes.bfloat16)


def whiten_kernel(windows, segs, pairs_ref, row_ref, traces_hbm, table_hbm, out_hbm, frames, table, sent, frame_sem, table_sem, sent_sem):
    channels = frames.shape[1]
    share = channels // segs // SPLIT
    loads = [
        pltpu.make_async_copy(traces_hbm.at[:, pl.ds(w * WIN, WIN)], frames.at[w], frame_sem.at[w])
        for w in range(windows)
    ]
    tables = [
        pltpu.make_async_copy(table_hbm.at[i], table.at[i], table_sem.at[i]) for i in range(PARITIES)
    ]
    per = GROUPS // PARITIES
    stores = [
        pltpu.make_async_copy(sent.at[pl.ds(i * per, per)], out_hbm.at[pl.ds(i * per, per)], sent_sem.at[i])
        for i in range(PARITIES)
    ]
    tables[0].start()
    for load in loads:
        load.start()
    tables[1].start()
    first_row = row_ref[pairs_ref[0, 0]].astype(jnp.float32)
    second_row = row_ref[pairs_ref[0, 1]].astype(jnp.float32)
    line = lax.broadcasted_iota(jnp.int32, (NOTE, BINS), 0)
    note = jnp.where(line == 0, first_row, second_row).astype(jnp.bfloat16)
    sent[:, :, :, 2 * windows * share :] = jnp.broadcast_to(note, (GROUPS, SPLIT, segs, NOTE, BINS))
    for load in loads:
        load.wait()
    for i in range(PARITIES):
        tables[i].wait()
        for w in range(windows):
            halves = jnp.concatenate((frames[w, :, :HALF], frames[w, :, HALF:]), axis=0)
            product = jnp.dot(halves, table[i], preferred_element_type=jnp.float32)
            first, second = product[:channels], product[channels:]
            spectra = first + second if i == 0 else first - second
            for k in range(per):
                real = spectra[:, 2 * k * BINS : (2 * k + 1) * BINS]
                imag = spectra[:, (2 * k + 1) * BINS : (2 * k + 2) * BINS]
                power = jnp.sum(real * real + imag * imag, axis=0, keepdims=True) * (1.0 / channels)
                gain = lax.rsqrt(power + 1e-06)
                for part, values in enumerate((real, imag)):
                    white = (values * gain).astype(jnp.bfloat16).reshape(segs, SPLIT, share, BINS)
                    at = (2 * w + part) * share
                    for h in range(SPLIT):
                        sent[i * per + k, h, :, at : at + share] = white[:, h]
        stores[i].start()
    for store in stores:
        store.wait()


def whiten(pairs, block_row, traces, windows, segs):
    channels = traces.shape[0]
    share = channels // segs // SPLIT
    shape = (GROUPS, SPLIT, segs, 2 * windows * share + NOTE, BINS)
    hbm = pl.BlockSpec(memory_space=pl.ANY)
    smem = pl.BlockSpec(memory_space=pltpu.SMEM)
    return pl.pallas_call(
        functools.partial(whiten_kernel, windows, segs),
        in_specs=[smem, smem, hbm, hbm],
        out_specs=hbm,
        out_shape=jax.ShapeDtypeStruct(shape, jnp.bfloat16),
        scratch_shapes=[
            pltpu.VMEM((windows, channels, WIN), jnp.bfloat16),
            pltpu.VMEM((PARITIES, HALF, NB), jnp.bfloat16),
            pltpu.VMEM(shape, jnp.bfloat16),
            pltpu.SemaphoreType.DMA((windows,)),
            pltpu.SemaphoreType.DMA((PARITIES,)),
            pltpu.SemaphoreType.DMA((PARITIES,)),
        ],
        compiler_params=pltpu.CompilerParams(vmem_limit_bytes=56 * 2**20),
        name="whiten",
    )(pairs, block_row, traces, jnp.asarray(forward_table()))


def cross_kernel(windows, spectra_ref, out_ref):
    segs = spectra_ref.shape[1]
    share = out_ref.shape[2]
    notes = [spectra_ref[i, 0, 2 * windows * share :].astype(jnp.float32) for i in range(out_ref.shape[0])]
    rows = [(note[0, 0].astype(jnp.int32), note[1, 0].astype(jnp.int32)) for note in notes]
    for i, (a, b) in enumerate(rows):
        real = jnp.zeros(out_ref.shape[2:], jnp.float32)
        imag = jnp.zeros(out_ref.shape[2:], jnp.float32)
        for s in range(segs):
            for w in range(windows):
                re = slice(2 * w * share, (2 * w + 1) * share)
                im = slice((2 * w + 1) * share, (2 * w + 2) * share)
                first_re = spectra_ref[a, s, re].astype(jnp.float32)
                first_im = spectra_ref[a, s, im].astype(jnp.float32)
                second_re = spectra_ref[b, s, re].astype(jnp.float32)
                second_im = spectra_ref[b, s, im].astype(jnp.float32)
                real += first_re * second_re + first_im * second_im
                imag += first_re * second_im - first_im * second_re
        out_ref[i, 0] = real.astype(jnp.bfloat16)
        out_ref[i, 1] = imag.astype(jnp.bfloat16)


def cross_groups(spectra, windows, share):
    vmem = pl.BlockSpec(memory_space=pltpu.VMEM)
    return pl.pallas_call(
        functools.partial(cross_kernel, windows),
        in_specs=[vmem],
        out_specs=vmem,
        out_shape=jax.ShapeDtypeStruct((spectra.shape[0], 2, share, BINS), jnp.bfloat16),
        compiler_params=pltpu.CompilerParams(vmem_limit_bytes=8 * 2**20),
        name="cross",
    )(spectra)


def cross_narrow(spectra, windows, share):
    parts, segs, rows, width = spectra.shape
    noted = spectra[:, 0, rows - NOTE : rows - NOTE + 2, 0].astype(jnp.int32)
    parted = spectra[:, :, : rows - NOTE].reshape(parts, segs * windows, 2, share, width)
    first = parted[noted[:, 0]].astype(jnp.float32)
    second = parted[noted[:, 1]].astype(jnp.float32)
    real = jnp.sum(first[:, :, 0] * second[:, :, 0] + first[:, :, 1] * second[:, :, 1], axis=1)
    imag = jnp.sum(first[:, :, 0] * second[:, :, 1] - first[:, :, 1] * second[:, :, 0], axis=1)
    return jnp.stack((real, imag), axis=1).astype(jnp.bfloat16)


def inverse_kernel(cross_ref, table_ref, out_ref):
    depth = NB

    def rows(parity):
        groups = range(parity * GROUPS // PARITIES, (parity + 1) * GROUPS // PARITIES)
        parts = [
            jnp.concatenate([cross_ref[g, h, part] for g in groups for part in range(2)], axis=1)
            for h in range(SPLIT)
        ]
        return jnp.concatenate(parts, axis=0)

    a = jnp.dot(rows(0), table_ref[:depth], preferred_element_type=jnp.float32)
    b = jnp.dot(rows(1), table_ref[depth:], preferred_element_type=jnp.float32)
    out_ref[0, :, : LAGS // 2] = a + b
    out_ref[0, :, LAGS // 2 :] = a - b


def inverse(cross, scale):
    vmem = pl.BlockSpec(memory_space=pltpu.VMEM)
    return pl.pallas_call(
        inverse_kernel,
        in_specs=[vmem, vmem],
        out_specs=vmem,
        out_shape=jax.ShapeDtypeStruct((1, SPLIT * cross.shape[3], LAGS), jnp.float32),
        compiler_params=pltpu.CompilerParams(vmem_limit_bytes=16 * 2**20),
        name="inverse",
    )(cross, jnp.asarray(inverse_table(scale)))


def local(traces, pairs, block_row):
    _, channels, samples = traces.shape
    windows = samples // WIN
    parts, segs = lax.axis_size("pair"), lax.axis_size("seg")
    per_group = parts // (GROUPS * SPLIT)
    share = channels // segs // SPLIT
    width = BINS // per_group
    rows = 2 * windows * share + NOTE
    sent = whiten(pairs, block_row, traces[0], windows, segs)
    if per_group > 1:
        sent = sent.reshape(GROUPS, SPLIT, segs, rows, per_group, width).transpose(0, 4, 1, 2, 3, 5)
    sent = sent.reshape(parts * segs, rows, width)
    held = lax.all_to_all(sent, ("pair", "seg"), split_axis=0, concat_axis=0, tiled=True)
    cross_of = cross_groups if per_group == 1 else cross_narrow
    cross = cross_of(held.reshape(parts, segs, rows, width), windows, share)
    mine = lax.all_to_all(cross, "pair", split_axis=0, concat_axis=0, tiled=True)
    mine = mine.reshape(GROUPS, per_group, SPLIT, 2, share, width)
    mine = mine.transpose(0, 2, 3, 4, 1, 5).reshape(GROUPS, SPLIT, 2, share, BINS)
    return inverse(mine, 1.0 / (windows * segs))


def solution(mesh):
    placed = (P("pair", None, "seg"), P("pair", None), P())
    return jax.shard_map(
        local, mesh=mesh, in_specs=placed, out_specs=P("pair", "seg", None), check_vma=False
    )
```

time: 188 us -> 53.9 us (0.29)
  other arithmetic: 38.3 us -> 0 us
  blocking collectives: 82.6 us -> 46.1 us
  waiting for transfers between devices: 24.2 us -> 0 us
  between operations: 13.6 us -> 0.02 us
  matrix products: 12.9 us -> 0 us
  local copies, waits for them, and re-layouts: 8.96 us -> 0.01 us
  Pallas kernels: 0 us -> 7.6 us
  starting transfers between devices: 7.32 us -> 0 us
    another operation x2 -> x0, other arithmetic: 35.6 us -> none
    all_gather x1 -> x0, blocking collectives: 31.5 us -> none  [local(): all_pairs = lax.all_gather(pairs, 'pair', axis=0, tiled=True)]
    reduce_scatter x1 -> x0, waiting for transfers between devices: 24.1 us -> none  [local(): lax.psum_scatter(correlated, 'seg', scatter_dimension=1, tiled=True)]
    dot_general x2 -> x0, matrix products: 12.9 us -> none  [the longest x1 9.08 us: local(): jnp.einsum('pskc,skl->pcl', cross, back, precision=lax.Precision.HIGHEST)]
    pallas_call x0 -> x3, Pallas kernels: none -> 7.6 us  [the longest x1 5.97 us: whiten(): pl.pallas_call(functools.partial(whiten_kernel, windows, segs), in_specs=...]
    all_to_all x1 -> x0, starting transfers between devices: 7.28 us -> none  [local(): lax.all_to_all(whitened, 'pair', split_axis=2, concat_axis=0, tiled=True)]
    all_to_all x1 -> x2, blocking collectives: 51.1 us -> 46.1 us  [the longest x1 36.7 us: local(): lax.all_to_all(sent, ('pair', 'seg'), split_axis=0, concat_axis=0, tiled=...]
    reshape x1 -> x0, local copies, waits for them, and re-layouts: 3.32 us -> none
  transfers between devices with their start and end apart: 2 -> 0, of which waited for: 1 -> 0; matrix products, arithmetic and copies ran while one was open for 1% -> 0% of each run, Pallas kernels for 0% -> 0%
where the time goes in v2:
time: 53.9 us; the launch traced here: 53.7 us
  blocking collectives  46.1 us (86%)
  Pallas kernels  7.6 us (14%)
    all_to_all x1, blocking collectives, local(): lax.all_to_all(sent, ('pair', 'seg'), split_axis=0, concat_axis=0, tiled=...  36.7 us
    all_to_all x1, blocking collectives, local(): lax.all_to_all(cross, 'pair', split_axis=0, concat_axis=0, tiled=True)  9.43 us
    pallas_call x1, Pallas kernels, whiten(): pl.pallas_call(functools.partial(whiten_kernel, windows, segs), in_specs=...  5.97 us
    pallas_call x1, Pallas kernels, inverse(): pl.pallas_call(inverse_kernel, in_specs=[vmem, vmem], out_specs=vmem, out...  1.18 us

profile of v2, /device:TPU:0, one launch (start us, length us, event | category | flops | bytes accessed | tf_op | source)
XLA Modules:
  0.0 53.7 jit_solution(13013176837664584133)
XLA Ops:
  0.0 6.0 %whiten.1 = bf16[4,2,4,136,128]{4,3,2,1,0:T(8,128)(2,1)} custom-call(s32[1,2]{1,0:T(1,128)} %pairs_ref.1, s32[8]{0:T(128)} %row_ref.1, bf16[128,8192]{1,0:T(8,128)(2,1)} %bitcast.7, bf16[2,1024,512]{2,1,0:T(8,128)(2,1)} %constant.4.clone.table_hbm), custom_call_target="tpu_custom_call" | custom-call | tf_op jit(solution)/shard_map/whiten/pallas_call | solution.py:96
  6.0 0.0 copy-start
  6.0 36.7 %all_to_all.10 = bf16[32,136,128]{2,1,0:T(8,128)(2,1)S(1)} all-to-all(bf16[32,136,128]{2,1,0:T(8,128)(2,1)} %bitcast.6), channel_id=1, replica_groups=mesh['pair'=8,'seg'=4] {'pair','seg'}, dimensions={0} | all-to-all | bytes 2228224 | tf_op jit(solution)/shard_map/all_to_all | solution.py:200
  42.7 0.5 cross.1
  43.1 9.4 %all_to_all.11 = bf16[8,2,16,128]{3,2,1,0:T(8,128)(2,1)S(1)} all-to-all(bf16[8,2,16,128]{3,2,1,0:T(8,128)(2,1)S(1)} %cross.1), channel_id=1, replica_groups=mesh['pair'=8,'seg'=4] {'pair'}, dimensions={0} | all-to-all | bytes 131072 | tf_op jit(solution)/shard_map/all_to_all | solution.py:203
  52.6 0.0 copy-done
  52.6 1.2 %inverse.1 = f32[1,32,2048]{2,1,0:T(8,128)} custom-call(bf16[4,2,2,16,128]{4,3,2,1,0:T(8,128)(2,1)S(1)} %bitcast.5, bf16[1024,1024]{1,0:T(8,128)(2,1)S(1)} %copy-done), custom_call_target="tpu_custom_call" | custom-call | tf_op jit(solution)/shard_map/inverse/pallas_call | solution.py:178
Async XLA Ops:
  6.0 46.6 %copy-start = (bf16[1024,1024]{1,0:T(8,128)(2,1)S(1)}, bf16[1024,1024]{1,0:T(8,128)(2,1)}, u32[]{:S(2)}) copy-start(bf16[1024,1024]{1,0:T(8,128)(2,1)} %constant.5.clone.table_ref) | copy-start | bytes 6291460

commit v3 on v2

--- a/solution.py
+++ b/solution.py
@@ -39,7 +39,7 @@
     return table.reshape(2 * NB, LAGS // 2).astype(ml_dtypes.bfloat16)
 
 
-def whiten_kernel(windows, segs, pairs_ref, row_ref, traces_hbm, table_hbm, out_hbm, frames, table, sent, frame_sem, table_sem, sent_sem):
+def whiten_kernel(windows, segs, pairs_hbm, row_hbm, traces_hbm, table_hbm, sent, pairs_ref, row_ref, frames, table, small_sem, frame_sem, table_sem):
     channels = frames.shape[1]
     share = channels // segs // SPLIT
     loads = [
@@ -50,21 +50,25 @@
         pltpu.make_async_copy(table_hbm.at[i], table.at[i], table_sem.at[i]) for i in range(PARITIES)
     ]
     per = GROUPS // PARITIES
-    stores = [
-        pltpu.make_async_copy(sent.at[pl.ds(i * per, per)], out_hbm.at[pl.ds(i * per, per)], sent_sem.at[i])
-        for i in range(PARITIES)
+    small = [
+        pltpu.make_async_copy(source, target, small_sem.at[k])
+        for k, (source, target) in enumerate(((pairs_hbm, pairs_ref), (row_hbm, row_ref)))
     ]
     tables[0].start()
     for load in loads:
         load.start()
     tables[1].start()
+    for load in small:
+        load.start()
+    for load in loads:
+        load.wait()
+    for load in small:
+        load.wait()
     first_row = row_ref[pairs_ref[0, 0]].astype(jnp.float32)
     second_row = row_ref[pairs_ref[0, 1]].astype(jnp.float32)
     line = lax.broadcasted_iota(jnp.int32, (NOTE, BINS), 0)
     note = jnp.where(line == 0, first_row, second_row).astype(jnp.bfloat16)
     sent[:, :, :, 2 * windows * share :] = jnp.broadcast_to(note, (GROUPS, SPLIT, segs, NOTE, BINS))
-    for load in loads:
-        load.wait()
     for i in range(PARITIES):
         tables[i].wait()
         for w in range(windows):
@@ -82,9 +86,10 @@
                     at = (2 * w + part) * share
                     for h in range(SPLIT):
                         sent[i * per + k, h, :, at : at + share] = white[:, h]
-        stores[i].start()
-    for store in stores:
-        store.wait()
+
+
+def in_hbm(values):
+    return pltpu.with_memory_space_constraint(values, pltpu.HBM)
 
 
 def whiten(pairs, block_row, traces, windows, segs):
@@ -92,23 +97,23 @@
     share = channels // segs // SPLIT
     shape = (GROUPS, SPLIT, segs, 2 * windows * share + NOTE, BINS)
     hbm = pl.BlockSpec(memory_space=pl.ANY)
-    smem = pl.BlockSpec(memory_space=pltpu.SMEM)
     return pl.pallas_call(
         functools.partial(whiten_kernel, windows, segs),
-        in_specs=[smem, smem, hbm, hbm],
-        out_specs=hbm,
-        out_shape=jax.ShapeDtypeStruct(shape, jnp.bfloat16),
+        in_specs=[hbm, hbm, hbm, hbm],
+        out_specs=pl.BlockSpec(memory_space=pltpu.VMEM),
+        out_shape=pltpu.VMEM(shape, jnp.bfloat16),
         scratch_shapes=[
+            pltpu.SMEM(pairs.shape, jnp.int32),
+            pltpu.SMEM(block_row.shape, jnp.int32),
             pltpu.VMEM((windows, channels, WIN), jnp.bfloat16),
             pltpu.VMEM((PARITIES, HALF, NB), jnp.bfloat16),
-            pltpu.VMEM(shape, jnp.bfloat16),
+            pltpu.SemaphoreType.DMA((2,)),
             pltpu.SemaphoreType.DMA((windows,)),
             pltpu.SemaphoreType.DMA((PARITIES,)),
-            pltpu.SemaphoreType.DMA((PARITIES,)),
         ],
-        compiler_params=pltpu.CompilerParams(vmem_limit_bytes=56 * 2**20),
+        compiler_params=pltpu.CompilerParams(vmem_limit_bytes=24 * 2**20),
         name="whiten",
-    )(pairs, block_row, traces, jnp.asarray(forward_table()))
+    )(*(in_hbm(values) for values in (pairs, block_row, traces, jnp.asarray(forward_table()))))
 
 
 def cross_kernel(windows, spectra_ref, out_ref):

time: 53.9 us -> 52.3 us (0.970)
  Pallas kernels: 7.6 us -> 6.15 us
    pallas_call x1, Pallas kernels: 5.97 us -> 4.52 us  [whiten(): pl.pallas_call(functools.partial(whiten_kernel, windows, segs), in_specs=...]
where the time goes in v3:
time: 52.3 us; the launch traced here: 52.1 us
  blocking collectives  45.9 us (88%)
  Pallas kernels  6.15 us (12%)
    all_to_all x1, blocking collectives, local(): lax.all_to_all(sent, ('pair', 'seg'), split_axis=0, concat_axis=0, tiled=...  36.5 us
    all_to_all x1, blocking collectives, local(): lax.all_to_all(cross, 'pair', split_axis=0, concat_axis=0, tiled=True)  9.43 us
    pallas_call x1, Pallas kernels, whiten(): pl.pallas_call(functools.partial(whiten_kernel, windows, segs), in_specs=...  4.52 us
    pallas_call x1, Pallas kernels, inverse(): pl.pallas_call(inverse_kernel, in_specs=[vmem, vmem], out_specs=vmem, out...  1.18 us

profile of v3, /device:TPU:0, one launch (start us, length us, event | category | flops | bytes accessed | tf_op | source)
XLA Modules:
  0.0 52.1 jit_solution(8289720178747119686)
XLA Ops:
  0.0 4.5 %whiten.1 = bf16[4,2,4,136,128]{4,3,2,1,0:T(8,128)(2,1)S(1)} custom-call(s32[1,2]{1,0:T(1,128)} %pairs_hbm.1, s32[8]{0:T(128)} %row_hbm.1, bf16[128,8192]{1,0:T(8,128)(2,1)} %bitcast.7, bf16[2,1024,512]{2,1,0:T(8,128)(2,1)} %constant.4.clone.table_hbm), custom_call_target="tpu_custom_call" | custom-call | tf_op jit(solution)/shard_map/whiten/pallas_call | solution.py:100
  4.5 0.0 copy-start
  4.5 36.5 %all_to_all.10 = bf16[32,136,128]{2,1,0:T(8,128)(2,1)S(1)} all-to-all(bf16[32,136,128]{2,1,0:T(8,128)(2,1)S(1)} %bitcast.4), channel_id=1, replica_groups=mesh['pair'=8,'seg'=4] {'pair','seg'}, dimensions={0} | all-to-all | bytes 2228224 | tf_op jit(solution)/shard_map/all_to_all | solution.py:205
  41.0 0.4 cross.1
  41.5 9.4 %all_to_all.11 = bf16[8,2,16,128]{3,2,1,0:T(8,128)(2,1)S(1)} all-to-all(bf16[8,2,16,128]{3,2,1,0:T(8,128)(2,1)S(1)} %cross.1), channel_id=1, replica_groups=mesh['pair'=8,'seg'=4] {'pair'}, dimensions={0} | all-to-all | bytes 131072 | tf_op jit(solution)/shard_map/all_to_all | solution.py:208
  50.9 0.0 copy-done
  50.9 1.2 %inverse.1 = f32[1,32,2048]{2,1,0:T(8,128)} custom-call(bf16[4,2,2,16,128]{4,3,2,1,0:T(8,128)(2,1)S(1)} %bitcast.6, bf16[1024,1024]{1,0:T(8,128)(2,1)S(1)} %copy-done), custom_call_target="tpu_custom_call" | custom-call | tf_op jit(solution)/shard_map/inverse/pallas_call | solution.py:183
Async XLA Ops:
  4.5 46.4 %copy-start = (bf16[1024,1024]{1,0:T(8,128)(2,1)S(1)}, bf16[1024,1024]{1,0:T(8,128)(2,1)}, u32[]{:S(2)}) copy-start(bf16[1024,1024]{1,0:T(8,128)(2,1)} %constant.5.clone.table_ref) | copy-start | bytes 6291460

commit v4 on v3

--- a/solution.py
+++ b/solution.py
@@ -49,43 +49,55 @@
     tables = [
         pltpu.make_async_copy(table_hbm.at[i], table.at[i], table_sem.at[i]) for i in range(PARITIES)
     ]
-    per = GROUPS // PARITIES
     small = [
         pltpu.make_async_copy(source, target, small_sem.at[k])
         for k, (source, target) in enumerate(((pairs_hbm, pairs_ref), (row_hbm, row_ref)))
     ]
+    per = GROUPS // PARITIES
     tables[0].start()
     for load in loads:
         load.start()
     tables[1].start()
     for load in small:
         load.start()
-    for load in loads:
-        load.wait()
+
+    def one(w, i):
+        halves = jnp.concatenate((frames[w, :, :HALF], frames[w, :, HALF:]), axis=0)
+        product = jnp.dot(halves, table[i], preferred_element_type=jnp.float32)
+        first, second = product[:channels], product[channels:]
+        spectra = first + second if i == 0 else first - second
+        for k in range(per):
+            real = spectra[:, 2 * k * BINS : (2 * k + 1) * BINS]
+            imag = spectra[:, (2 * k + 1) * BINS : (2 * k + 2) * BINS]
+            power = jnp.sum(real * real + imag * imag, axis=0, keepdims=True) * (1.0 / channels)
+            gain = lax.rsqrt(power + 1e-06)
+            for part, values in enumerate((real, imag)):
+                white = (values * gain).astype(jnp.bfloat16).reshape(segs, SPLIT, share, BINS)
+                at = (2 * w + part) * share
+                for h in range(SPLIT):
+                    sent[i * per + k, h, :, at : at + share] = white[:, h]
+
+    early = windows // 2
+    tables[0].wait()
+    for w in range(early):
+        loads[w].wait()
+    for w in range(early):
+        one(w, 0)
+    for w in range(early, windows):
+        loads[w].wait()
+    tables[1].wait()
     for load in small:
         load.wait()
-    first_row = row_ref[pairs_ref[0, 0]].astype(jnp.float32)
-    second_row = row_ref[pairs_ref[0, 1]].astype(jnp.float32)
+    parts = row_ref.shape[0]
+    first_row = ((row_ref[pairs_ref[0, 0]] + parts // 2) % parts).astype(jnp.float32)
+    second_row = ((row_ref[pairs_ref[0, 1]] + parts // 2) % parts).astype(jnp.float32)
     line = lax.broadcasted_iota(jnp.int32, (NOTE, BINS), 0)
     note = jnp.where(line == 0, first_row, second_row).astype(jnp.bfloat16)
     sent[:, :, :, 2 * windows * share :] = jnp.broadcast_to(note, (GROUPS, SPLIT, segs, NOTE, BINS))
-    for i in range(PARITIES):
-        tables[i].wait()
-        for w in range(windows):
-            halves = jnp.concatenate((frames[w, :, :HALF], frames[w, :, HALF:]), axis=0)
-            product = jnp.dot(halves, table[i], preferred_element_type=jnp.float32)
-            first, second = product[:channels], product[channels:]
-            spectra = first + second if i == 0 else first - second
-            for k in range(per):
-                real = spectra[:, 2 * k * BINS : (2 * k + 1) * BINS]
-                imag = spectra[:, (2 * k + 1) * BINS : (2 * k + 2) * BINS]
-                power = jnp.sum(real * real + imag * imag, axis=0, keepdims=True) * (1.0 / channels)
-                gain = lax.rsqrt(power + 1e-06)
-                for part, values in enumerate((real, imag)):
-                    white = (values * gain).astype(jnp.bfloat16).reshape(segs, SPLIT, share, BINS)
-                    at = (2 * w + part) * share
-                    for h in range(SPLIT):
-                        sent[i * per + k, h, :, at : at + share] = white[:, h]
+    for w in range(early, windows):
+        one(w, 0)
+    for w in range(windows):
+        one(w, 1)
 
 
 def in_hbm(values):
@@ -190,6 +202,10 @@
     )(cross, jnp.asarray(inverse_table(scale)))
 
 
+def exchange_order(parts):
+    return [(i + parts // 2) % parts for i in range(parts)]
+
+
 def local(traces, pairs, block_row):
     _, channels, samples = traces.shape
     windows = samples // WIN
@@ -202,10 +218,16 @@
     if per_group > 1:
         sent = sent.reshape(GROUPS, SPLIT, segs, rows, per_group, width).transpose(0, 4, 1, 2, 3, 5)
     sent = sent.reshape(parts * segs, rows, width)
-    held = lax.all_to_all(sent, ("pair", "seg"), split_axis=0, concat_axis=0, tiled=True)
+    order = exchange_order(parts)
+    everyone = [i * segs + s for i in order for s in range(segs)]
+    held = lax.all_to_all(
+        sent, ("pair", "seg"), split_axis=0, concat_axis=0, tiled=True, axis_index_groups=[everyone]
+    )
     cross_of = cross_groups if per_group == 1 else cross_narrow
     cross = cross_of(held.reshape(parts, segs, rows, width), windows, share)
-    mine = lax.all_to_all(cross, "pair", split_axis=0, concat_axis=0, tiled=True)
+    mine = lax.all_to_all(
+        cross, "pair", split_axis=0, concat_axis=0, tiled=True, axis_index_groups=[order]
+    )
     mine = mine.reshape(GROUPS, per_group, SPLIT, 2, share, width)
     mine = mine.transpose(0, 2, 3, 4, 1, 5).reshape(GROUPS, SPLIT, 2, share, BINS)
     return inverse(mine, 1.0 / (windows * segs))

time: 52.3 us -> 51.1 us (0.977)
  blocking collectives: 45.9 us -> 45 us
    all_to_all x1, blocking collectives: 9.43 us -> 8.55 us  [local(): lax.all_to_all(cross, 'pair', split_axis=0, concat_axis=0, tiled=True, ax...]
where the time goes in v4:
time: 51.1 us; the launch traced here: 50.9 us
  blocking collectives  45 us (88%)
  Pallas kernels  5.85 us (11%)
    all_to_all x1, blocking collectives, local(): lax.all_to_all(sent, ('pair', 'seg'), split_axis=0, concat_axis=0, tiled=...  36.5 us
    all_to_all x1, blocking collectives, local(): lax.all_to_all(cross, 'pair', split_axis=0, concat_axis=0, tiled=True, ax...  8.55 us
    pallas_call x1, Pallas kernels, whiten(): pl.pallas_call(functools.partial(whiten_kernel, windows, segs), in_specs=...  4.23 us
    pallas_call x1, Pallas kernels, inverse(): pl.pallas_call(inverse_kernel, in_specs=[vmem, vmem], out_specs=vmem, out...  1.18 us

profile of v4, /device:TPU:0, one launch (start us, length us, event | category | flops | bytes accessed | tf_op | source)
XLA Modules:
  0.0 50.9 jit_solution(5988060865911646520)
XLA Ops:
  0.0 4.2 %whiten.1 = bf16[4,2,4,136,128]{4,3,2,1,0:T(8,128)(2,1)S(1)} custom-call(s32[1,2]{1,0:T(1,128)} %pairs_hbm.1, s32[8]{0:T(128)} %row_hbm.1, bf16[128,8192]{1,0:T(8,128)(2,1)} %bitcast.7, bf16[2,1024,512]{2,1,0:T(8,128)(2,1)} %constant.4.clone.table_hbm), custom_call_target="tpu_custom_call" | custom-call | tf_op jit(solution)/shard_map/whiten/pallas_call | solution.py:112
  4.2 0.0 copy-start
  4.2 36.5 %all_to_all.10 = bf16[32,136,128]{2,1,0:T(8,128)(2,1)S(1)} all-to-all(bf16[32,136,128]{2,1,0:T(8,128)(2,1)S(1)} %bitcast.4), channel_id=1, replica_groups={{16,17,18,19,20,21,22,23,24,25,26,27,28,29,30,31,0,1,2,3,4,5,6,7,8,9,10..., dimensions={0} | all-to-all | bytes 2228224 | tf_op jit(solution)/shard_map/all_to_all | solution.py:223
  40.7 0.4 cross.1
  41.2 8.6 %all_to_all.11 = bf16[8,2,16,128]{3,2,1,0:T(8,128)(2,1)S(1)} all-to-all(bf16[8,2,16,128]{3,2,1,0:T(8,128)(2,1)S(1)} %cross.1), channel_id=1, replica_groups={{16,20,24,28,0,4,8,12},{17,21,25,29,1,5,9,13},{18,22,26,30,2,6,10,14},{..., dimensions={0} | all-to-all | bytes 131072 | tf_op jit(solution)/shard_map/all_to_all | solution.py:228
  49.7 0.0 copy-done
  49.7 1.2 %inverse.1 = f32[1,32,2048]{2,1,0:T(8,128)} custom-call(bf16[4,2,2,16,128]{4,3,2,1,0:T(8,128)(2,1)S(1)} %bitcast.6, bf16[1024,1024]{1,0:T(8,128)(2,1)S(1)} %copy-done), custom_call_target="tpu_custom_call" | custom-call | tf_op jit(solution)/shard_map/inverse/pallas_call | solution.py:195
Async XLA Ops:
  4.2 45.5 %copy-start = (bf16[1024,1024]{1,0:T(8,128)(2,1)S(1)}, bf16[1024,1024]{1,0:T(8,128)(2,1)}, u32[]{:S(2)}) copy-start(bf16[1024,1024]{1,0:T(8,128)(2,1)} %constant.5.clone.table_ref) | copy-start | bytes 6291460

commit v5 on v4

v5 whole, which is shorter than its diff:
```python
import functools

import jax
import jax.numpy as jnp
import ml_dtypes
import numpy as np
from jax import lax
from jax.experimental import pallas as pl
from jax.experimental.pallas import tpu as pltpu
from jax.sharding import PartitionSpec as P

WIN = 2048
NB = 512
LAGS = 2048
HALF = WIN // 2
BINS = 128
GROUPS = NB // BINS
SPLIT = 2
PARITIES = 2
NOTE = 8
NEAR = 2


def frequencies():
    even = np.arange(2, NB + 1, 2)
    odd = np.arange(1, NB + 1, 2)
    return np.concatenate((even, odd)).reshape(GROUPS, BINS)


def forward_table():
    phase = (frequencies()[:, :, None] * np.arange(HALF) % WIN) * (2.0 * np.pi / WIN)
    table = np.stack((np.cos(phase), -np.sin(phase)), axis=1).reshape(PARITIES, NB, HALF)
    return np.ascontiguousarray(table.transpose(0, 2, 1)).astype(ml_dtypes.bfloat16)


def inverse_table(scale):
    shifts = np.arange(LAGS // 2) - LAGS // 2
    phase = (frequencies()[:, :, None] * shifts % WIN) * (2.0 * np.pi / WIN)
    table = np.stack((np.cos(phase), -np.sin(phase)), axis=1) * scale
    return table.reshape(2 * NB, LAGS // 2).astype(ml_dtypes.bfloat16)


def whiten_kernel(windows, far, near, pairs_hbm, row_hbm, traces_hbm, table_hbm, sent, pairs_ref, row_ref, frames, table, small_sem, frame_sem, table_sem):
    channels = frames.shape[1]
    share = channels // (far * near * SPLIT)
    loads = [
        pltpu.make_async_copy(traces_hbm.at[:, pl.ds(w * WIN, WIN)], frames.at[w], frame_sem.at[w])
        for w in range(windows)
    ]
    tables = [
        pltpu.make_async_copy(table_hbm.at[i], table.at[i], table_sem.at[i]) for i in range(PARITIES)
    ]
    small = [
        pltpu.make_async_copy(source, target, small_sem.at[k])
        for k, (source, target) in enumerate(((pairs_hbm, pairs_ref), (row_hbm, row_ref)))
    ]
    per = GROUPS // PARITIES
    tables[0].start()
    for load in loads:
        load.start()
    tables[1].start()
    for load in small:
        load.start()

    def one(w, i):
        halves = jnp.concatenate((frames[w, :, :HALF], frames[w, :, HALF:]), axis=0)
        product = jnp.dot(halves, table[i], preferred_element_type=jnp.float32)
        first, second = product[:channels], product[channels:]
        spectra = first + second if i == 0 else first - second
        for k in range(per):
            real = spectra[:, 2 * k * BINS : (2 * k + 1) * BINS]
            imag = spectra[:, (2 * k + 1) * BINS : (2 * k + 2) * BINS]
            power = jnp.sum(real * real + imag * imag, axis=0, keepdims=True) * (1.0 / channels)
            gain = lax.rsqrt(power + 1e-06)
            for part, values in enumerate((real, imag)):
                white = (values * gain).astype(jnp.bfloat16).reshape(far, near, SPLIT, share, BINS)
                for f in range(far):
                    at = (2 * (f * windows + w) + part) * share
                    for h in range(SPLIT):
                        sent[i * per + k, h, :, at : at + share] = white[f, :, h]

    early = windows // 2
    tables[0].wait()
    for w in range(early):
        loads[w].wait()
    for w in range(early):
        one(w, 0)
    for w in range(early, windows):
        loads[w].wait()
    tables[1].wait()
    for load in small:
        load.wait()
    parts = row_ref.shape[0]
    first_row = ((row_ref[pairs_ref[0, 0]] + parts // 2) % parts).astype(jnp.float32)
    second_row = ((row_ref[pairs_ref[0, 1]] + parts // 2) % parts).astype(jnp.float32)
    line = lax.broadcasted_iota(jnp.int32, (NOTE, BINS), 0)
    note = jnp.where(line == 0, first_row, second_row).astype(jnp.bfloat16)
    sent[:, :, :, 2 * far * windows * share :] = jnp.broadcast_to(note, (GROUPS, SPLIT, near, NOTE, BINS))
    for w in range(early, windows):
        one(w, 0)
    for w in range(windows):
        one(w, 1)


def in_hbm(values):
    return pltpu.with_memory_space_constraint(values, pltpu.HBM)


def whiten(pairs, block_row, traces, windows, far, near):
    channels = traces.shape[0]
    share = channels // (far * near * SPLIT)
    shape = (GROUPS, SPLIT, near, 2 * far * windows * share + NOTE, BINS)
    hbm = pl.BlockSpec(memory_space=pl.ANY)
    return pl.pallas_call(
        functools.partial(whiten_kernel, windows, far, near),
        in_specs=[hbm, hbm, hbm, hbm],
        out_specs=pl.BlockSpec(memory_space=pltpu.VMEM),
        out_shape=pltpu.VMEM(shape, jnp.bfloat16),
        scratch_shapes=[
            pltpu.SMEM(pairs.shape, jnp.int32),
            pltpu.SMEM(block_row.shape, jnp.int32),
            pltpu.VMEM((windows, channels, WIN), jnp.bfloat16),
            pltpu.VMEM((PARITIES, HALF, NB), jnp.bfloat16),
            pltpu.SemaphoreType.DMA((2,)),
            pltpu.SemaphoreType.DMA((windows,)),
            pltpu.SemaphoreType.DMA((PARITIES,)),
        ],
        compiler_params=pltpu.CompilerParams(vmem_limit_bytes=24 * 2**20),
        name="whiten",
    )(*(in_hbm(values) for values in (pairs, block_row, traces, jnp.asarray(forward_table()))))


def cross_kernel(windows, spectra_ref, out_ref):
    count, far, _, share, _ = out_ref.shape
    near = spectra_ref.shape[1]
    notes = [spectra_ref[i, 0, 2 * far * windows * share :].astype(jnp.float32) for i in range(count)]
    rows = [(note[0, 0].astype(jnp.int32), note[1, 0].astype(jnp.int32)) for note in notes]
    for i, (a, b) in enumerate(rows):
        for f in range(far):
            real = jnp.zeros(out_ref.shape[3:], jnp.float32)
            imag = jnp.zeros(out_ref.shape[3:], jnp.float32)
            for n in range(near):
                for w in range(windows):
                    at = 2 * (f * windows + w) * share
                    re, im = slice(at, at + share), slice(at + share, at + 2 * share)
                    first_re = spectra_ref[a, n, re].astype(jnp.float32)
                    first_im = spectra_ref[a, n, im].astype(jnp.float32)
                    second_re = spectra_ref[b, n, re].astype(jnp.float32)
                    second_im = spectra_ref[b, n, im].astype(jnp.float32)
                    real += first_re * second_re + first_im * second_im
                    imag += first_re * second_im - first_im * second_re
            out_ref[i, f, 0] = real.astype(jnp.bfloat16)
            out_ref[i, f, 1] = imag.astype(jnp.bfloat16)


def cross_groups(spectra, windows, far, share):
    vmem = pl.BlockSpec(memory_space=pltpu.VMEM)
    return pl.pallas_call(
        functools.partial(cross_kernel, windows),
        in_specs=[vmem],
        out_specs=vmem,
        out_shape=jax.ShapeDtypeStruct((spectra.shape[0], far, 2, share, BINS), jnp.bfloat16),
        compiler_params=pltpu.CompilerParams(vmem_limit_bytes=8 * 2**20),
        name="cross",
    )(spectra)


def cross_narrow(spectra, windows, far, share):
    parts, near, rows, width = spectra.shape
    noted = spectra[:, 0, rows - NOTE : rows - NOTE + 2, 0].astype(jnp.int32)
    parted = spectra[:, :, : rows - NOTE].reshape(parts, near, far, windows, 2, share, width)
    first = parted[noted[:, 0]].astype(jnp.float32)
    second = parted[noted[:, 1]].astype(jnp.float32)
    first_re, first_im, second_re, second_im = first[..., 0, :, :], first[..., 1, :, :], second[..., 0, :, :], second[..., 1, :, :]
    real = jnp.sum(first_re * second_re + first_im * second_im, axis=(1, 3))
    imag = jnp.sum(first_re * second_im - first_im * second_re, axis=(1, 3))
    return jnp.stack((real, imag), axis=2).astype(jnp.bfloat16)


def inverse_kernel(cross_ref, table_ref, out_ref):
    depth = NB
    far, share = cross_ref.shape[2], cross_ref.shape[4]

    def lags(parity):
        groups = range(parity * GROUPS // PARITIES, (parity + 1) * GROUPS // PARITIES)
        parts = [
            jnp.concatenate([cross_ref[g, h, f, part] for g in groups for part in range(2)], axis=1)
            for f in range(far)
            for h in range(SPLIT)
        ]
        table = table_ref[parity * depth : (parity + 1) * depth]
        product = jnp.dot(jnp.concatenate(parts, axis=0), table, preferred_element_type=jnp.float32)
        return sum(product[f * SPLIT * share : (f + 1) * SPLIT * share] for f in range(far))

    a, b = lags(0), lags(1)
    out_ref[0, :, : LAGS // 2] = a + b
    out_ref[0, :, LAGS // 2 :] = a - b


def inverse(cross, scale):
    vmem = pl.BlockSpec(memory_space=pltpu.VMEM)
    return pl.pallas_call(
        inverse_kernel,
        in_specs=[vmem, vmem],
        out_specs=vmem,
        out_shape=jax.ShapeDtypeStruct((1, SPLIT * cross.shape[4], LAGS), jnp.float32),
        compiler_params=pltpu.CompilerParams(vmem_limit_bytes=16 * 2**20),
        name="inverse",
    )(cross, jnp.asarray(inverse_table(scale)))


def exchange_order(parts):
    return [(i + parts // 2) % parts for i in range(parts)]


def all_to_all(sent, order, axis):
    size = lax.axis_size(axis)
    group = [i * size + k for i in order for k in range(size)]
    return lax.all_to_all(
        sent, ("pair", axis), split_axis=0, concat_axis=0, tiled=True, axis_index_groups=[group]
    )


def local(traces, pairs, block_row):
    _, channels, samples = traces.shape
    windows = samples // WIN
    parts, far, near = lax.axis_size("pair"), lax.axis_size("far"), lax.axis_size("near")
    per_group = parts // (GROUPS * SPLIT)
    share = channels // (far * near * SPLIT)
    width = BINS // per_group
    rows = 2 * far * windows * share + NOTE
    sent = whiten(pairs, block_row, traces[0], windows, far, near)
    if per_group > 1:
        sent = sent.reshape(GROUPS, SPLIT, near, rows, per_group, width).transpose(0, 4, 1, 2, 3, 5)
    order = exchange_order(parts)
    held = all_to_all(sent.reshape(parts * near, rows, width), order, "near")
    cross_of = cross_groups if per_group == 1 else cross_narrow
    cross = cross_of(held.reshape(parts, near, rows, width), windows, far, share)
    mine = all_to_all(cross.reshape(parts * far, 2, share, width), order, "far")
    mine = mine.reshape(GROUPS, per_group, SPLIT, far, 2, share, width)
    mine = mine.transpose(0, 2, 3, 4, 5, 1, 6).reshape(GROUPS, SPLIT, far, 2, share, BINS)
    return inverse(mine, 1.0 / (windows * far * near))


def solution(mesh):
    pairs, segs = mesh.devices.shape
    split = jax.sharding.Mesh(mesh.devices.reshape(pairs, segs // NEAR, NEAR), ("pair", "far", "near"))
    placed = (P("pair", None, ("far", "near")), P("pair", None), P())
    return jax.shard_map(
        local, mesh=split, in_specs=placed, out_specs=P("pair", ("far", "near"), None), check_vma=False
    )
```

time: 51.1 us -> 50.1 us (0.980)
  blocking collectives: 45 us -> 44 us
    all_to_all x2, blocking collectives: 45 us -> 44 us  [all_to_all(): lax.all_to_all(sent, ('pair', axis), split_axis=0, concat_axis=0, tiled=T...]
where the time goes in v5:
time: 50.1 us; the launch traced here: 49.9 us
  blocking collectives  44 us (88%)
  Pallas kernels  5.86 us (12%)
    all_to_all x2, blocking collectives, all_to_all(): lax.all_to_all(sent, ('pair', axis), split_axis=0, concat_axis=0, tiled=T...  44 us
    pallas_call x1, Pallas kernels, whiten(): pl.pallas_call(functools.partial(whiten_kernel, windows, far, near), in_s...  4.23 us
    pallas_call x1, Pallas kernels, inverse(): pl.pallas_call(inverse_kernel, in_specs=[vmem, vmem], out_specs=vmem, out...  1.19 us

profile of v5, /device:TPU:0, one launch (start us, length us, event | category | flops | bytes accessed | tf_op | source)
XLA Modules:
  0.0 49.9 jit_solution(5497257391600751207)
XLA Ops:
  0.0 4.2 %whiten.1 = bf16[4,2,2,264,128]{4,3,2,1,0:T(8,128)(2,1)S(1)} custom-call(s32[1,2]{1,0:T(1,128)} %pairs_hbm.1, s32[8]{0:T(128)} %row_hbm.1, bf16[128,8192]{1,0:T(8,128)(2,1)} %bitcast.9, bf16[2,1024,512]{2,1,0:T(8,128)(2,1)} %constant.4.clone.table_hbm), custom_call_target="tpu_custom_call" | custom-call | tf_op jit(solution)/shard_map/whiten/pallas_call | solution.py:114
  4.2 0.0 copy-start
  4.2 33.5 %all_to_all.10 = bf16[16,264,128]{2,1,0:T(8,128)(2,1)S(1)} all-to-all(bf16[16,264,128]{2,1,0:T(8,128)(2,1)S(1)} %bitcast.6), channel_id=1, replica_groups={{16,17,20,21,24,25,28,29,0,1,4,5,8,9,12,13},{18,19,22,23,26,27,30,31,2,..., dimensions={0} | all-to-all | bytes 2162688 | tf_op jit(solution)/shard_map/all_to_all | solution.py:219
  37.7 0.4 cross.1
  38.2 10.5 %all_to_all.11 = bf16[16,2,16,128]{3,2,1,0:T(8,128)(2,1)S(1)} all-to-all(bf16[16,2,16,128]{3,2,1,0:T(8,128)(2,1)S(1)} %bitcast.8), channel_id=1, replica_groups={{16,18,20,22,24,26,28,30,0,2,4,6,8,10,12,14},{17,19,21,23,25,27,29,31,1..., dimensions={0} | all-to-all | bytes 262144 | tf_op jit(solution)/shard_map/all_to_all | solution.py:219
  48.7 0.0 copy-done
  48.7 1.2 %inverse.1 = f32[1,32,2048]{2,1,0:T(8,128)} custom-call(bf16[4,2,2,2,16,128]{5,4,3,2,1,0:T(8,128)(2,1)S(1)} %bitcast.7, bf16[1024,1024]{1,0:T(8,128)(2,1)S(1)} %copy-done), custom_call_target="tpu_custom_call" | custom-call | tf_op jit(solution)/shard_map/inverse/pallas_call | solution.py:202
Async XLA Ops:
  4.2 44.5 %copy-start = (bf16[1024,1024]{1,0:T(8,128)(2,1)S(1)}, bf16[1024,1024]{1,0:T(8,128)(2,1)}, u32[]{:S(2)}) copy-start(bf16[1024,1024]{1,0:T(8,128)(2,1)} %constant.5.clone.table_ref) | copy-start | bytes 6291460

commit v6 on v5

--- a/solution.py
+++ b/solution.py
@@ -77,7 +77,8 @@
                 for f in range(far):
                     at = (2 * (f * windows + w) + part) * share
                     for h in range(SPLIT):
-                        sent[i * per + k, h, :, at : at + share] = white[f, :, h]
+                        for n in range(near):
+                            sent[i * per + k, h, near - 1 - n, at : at + share] = white[f, n, h]
 
     early = windows // 2
     tables[0].wait()
@@ -90,9 +91,9 @@
     tables[1].wait()
     for load in small:
         load.wait()
-    parts = row_ref.shape[0]
-    first_row = ((row_ref[pairs_ref[0, 0]] + parts // 2) % parts).astype(jnp.float32)
-    second_row = ((row_ref[pairs_ref[0, 1]] + parts // 2) % parts).astype(jnp.float32)
+    turn = row_ref.shape[0] // 2 + 1
+    first_row = (row_ref[pairs_ref[0, 0]] ^ turn).astype(jnp.float32)
+    second_row = (row_ref[pairs_ref[0, 1]] ^ turn).astype(jnp.float32)
     line = lax.broadcasted_iota(jnp.int32, (NOTE, BINS), 0)
     note = jnp.where(line == 0, first_row, second_row).astype(jnp.bfloat16)
     sent[:, :, :, 2 * far * windows * share :] = jnp.broadcast_to(note, (GROUPS, SPLIT, near, NOTE, BINS))
@@ -149,8 +150,8 @@
                     second_im = spectra_ref[b, n, im].astype(jnp.float32)
                     real += first_re * second_re + first_im * second_im
                     imag += first_re * second_im - first_im * second_re
-            out_ref[i, f, 0] = real.astype(jnp.bfloat16)
-            out_ref[i, f, 1] = imag.astype(jnp.bfloat16)
+            out_ref[i, far - 1 - f, 0] = real.astype(jnp.bfloat16)
+            out_ref[i, far - 1 - f, 1] = imag.astype(jnp.bfloat16)
 
 
 def cross_groups(spectra, windows, far, share):
@@ -174,7 +175,7 @@
     first_re, first_im, second_re, second_im = first[..., 0, :, :], first[..., 1, :, :], second[..., 0, :, :], second[..., 1, :, :]
     real = jnp.sum(first_re * second_re + first_im * second_im, axis=(1, 3))
     imag = jnp.sum(first_re * second_im - first_im * second_re, axis=(1, 3))
-    return jnp.stack((real, imag), axis=2).astype(jnp.bfloat16)
+    return jnp.stack((real, imag), axis=2)[:, ::-1].astype(jnp.bfloat16)
 
 
 def inverse_kernel(cross_ref, table_ref, out_ref):
@@ -210,12 +211,12 @@
 
 
 def exchange_order(parts):
-    return [(i + parts // 2) % parts for i in range(parts)]
+    return [i ^ (parts // 2 + 1) for i in range(parts)]
 
 
 def all_to_all(sent, order, axis):
     size = lax.axis_size(axis)
-    group = [i * size + k for i in order for k in range(size)]
+    group = [i * size + size - 1 - k for i in order for k in range(size)]
     return lax.all_to_all(
         sent, ("pair", axis), split_axis=0, concat_axis=0, tiled=True, axis_index_groups=[group]
     )

time: 50.1 us -> 48.1 us (0.960)
  blocking collectives: 44 us -> 42.1 us
    all_to_all x2, blocking collectives: 44 us -> 42.1 us  [all_to_all(): lax.all_to_all(sent, ('pair', axis), split_axis=0, concat_axis=0, tiled=T...]
where the time goes in v6:
time: 48.1 us; the launch traced here: 48 us
  blocking collectives  42.1 us (88%)
  Pallas kernels  5.86 us (12%)
    all_to_all x2, blocking collectives, all_to_all(): lax.all_to_all(sent, ('pair', axis), split_axis=0, concat_axis=0, tiled=T...  42.1 us
    pallas_call x1, Pallas kernels, whiten(): pl.pallas_call(functools.partial(whiten_kernel, windows, far, near), in_s...  4.23 us
    pallas_call x1, Pallas kernels, inverse(): pl.pallas_call(inverse_kernel, in_specs=[vmem, vmem], out_specs=vmem, out...  1.19 us

profile of v6, /device:TPU:0, one launch (start us, length us, event | category | flops | bytes accessed | tf_op | source)
XLA Modules:
  0.0 48.0 jit_solution(4047364628476874010)
XLA Ops:
  0.0 4.2 %whiten.1 = bf16[4,2,2,264,128]{4,3,2,1,0:T(8,128)(2,1)S(1)} custom-call(s32[1,2]{1,0:T(1,128)} %pairs_hbm.1, s32[8]{0:T(128)} %row_hbm.1, bf16[128,8192]{1,0:T(8,128)(2,1)} %bitcast.9, bf16[2,1024,512]{2,1,0:T(8,128)(2,1)} %constant.4.clone.table_hbm), custom_call_target="tpu_custom_call" | custom-call | tf_op jit(solution)/shard_map/whiten/pallas_call | solution.py:115
  4.2 0.0 copy-start
  4.2 32.3 %all_to_all.10 = bf16[16,264,128]{2,1,0:T(8,128)(2,1)S(1)} all-to-all(bf16[16,264,128]{2,1,0:T(8,128)(2,1)S(1)} %bitcast.6), channel_id=1, replica_groups={{21,20,17,16,29,28,25,24,5,4,1,0,13,12,9,8},{23,22,19,18,31,30,27,26,7,..., dimensions={0} | all-to-all | bytes 2162688 | tf_op jit(solution)/shard_map/all_to_all | solution.py:220
  36.5 0.4 cross.1
  37.0 9.8 %all_to_all.11 = bf16[16,2,16,128]{3,2,1,0:T(8,128)(2,1)S(1)} all-to-all(bf16[16,2,16,128]{3,2,1,0:T(8,128)(2,1)S(1)} %bitcast.8), channel_id=1, replica_groups={{22,20,18,16,30,28,26,24,6,4,2,0,14,12,10,8},{23,21,19,17,31,29,27,25,7..., dimensions={0} | all-to-all | bytes 262144 | tf_op jit(solution)/shard_map/all_to_all | solution.py:220
  46.8 0.0 copy-done
  46.8 1.2 %inverse.1 = f32[1,32,2048]{2,1,0:T(8,128)} custom-call(bf16[4,2,2,2,16,128]{5,4,3,2,1,0:T(8,128)(2,1)S(1)} %bitcast.7, bf16[1024,1024]{1,0:T(8,128)(2,1)S(1)} %copy-done), custom_call_target="tpu_custom_call" | custom-call | tf_op jit(solution)/shard_map/inverse/pallas_call | solution.py:203
Async XLA Ops:
  4.2 42.5 %copy-start = (bf16[1024,1024]{1,0:T(8,128)(2,1)S(1)}, bf16[1024,1024]{1,0:T(8,128)(2,1)}, u32[]{:S(2)}) copy-start(bf16[1024,1024]{1,0:T(8,128)(2,1)} %constant.5.clone.table_ref) | copy-start | bytes 6291460

commit v7 on v6

--- a/solution.py
+++ b/solution.py
@@ -18,7 +18,7 @@
 SPLIT = 2
 PARITIES = 2
 NOTE = 8
-NEAR = 2
+OUTER = 2
 
 
 def frequencies():
@@ -40,9 +40,9 @@
     return table.reshape(2 * NB, LAGS // 2).astype(ml_dtypes.bfloat16)
 
 
-def whiten_kernel(windows, far, near, pairs_hbm, row_hbm, traces_hbm, table_hbm, sent, pairs_ref, row_ref, frames, table, small_sem, frame_sem, table_sem):
+def whiten_kernel(windows, inner, outer, pairs_hbm, row_hbm, traces_hbm, table_hbm, sent, pairs_ref, row_ref, frames, table, small_sem, frame_sem, table_sem):
     channels = frames.shape[1]
-    share = channels // (far * near * SPLIT)
+    share = channels // (inner * outer * SPLIT)
     loads = [
         pltpu.make_async_copy(traces_hbm.at[:, pl.ds(w * WIN, WIN)], frames.at[w], frame_sem.at[w])
         for w in range(windows)
@@ -73,12 +73,12 @@
             power = jnp.sum(real * real + imag * imag, axis=0, keepdims=True) * (1.0 / channels)
             gain = lax.rsqrt(power + 1e-06)
             for part, values in enumerate((real, imag)):
-                white = (values * gain).astype(jnp.bfloat16).reshape(far, near, SPLIT, share, BINS)
-                for f in range(far):
+                white = (values * gain).astype(jnp.bfloat16).reshape(outer, inner, SPLIT, share, BINS)
+                for f in range(inner):
                     at = (2 * (f * windows + w) + part) * share
                     for h in range(SPLIT):
-                        for n in range(near):
-                            sent[i * per + k, h, near - 1 - n, at : at + share] = white[f, n, h]
+                        for n in range(outer):
+                            sent[i * per + k, h, outer - 1 - n, at : at + share] = white[n, f, h]
 
     early = windows // 2
     tables[0].wait()
@@ -96,7 +96,7 @@
     second_row = (row_ref[pairs_ref[0, 1]] ^ turn).astype(jnp.float32)
     line = lax.broadcasted_iota(jnp.int32, (NOTE, BINS), 0)
     note = jnp.where(line == 0, first_row, second_row).astype(jnp.bfloat16)
-    sent[:, :, :, 2 * far * windows * share :] = jnp.broadcast_to(note, (GROUPS, SPLIT, near, NOTE, BINS))
+    sent[:, :, :, 2 * inner * windows * share :] = jnp.broadcast_to(note, (GROUPS, SPLIT, outer, NOTE, BINS))
     for w in range(early, windows):
         one(w, 0)
     for w in range(windows):
@@ -107,13 +107,13 @@
     return pltpu.with_memory_space_constraint(values, pltpu.HBM)
 
 
-def whiten(pairs, block_row, traces, windows, far, near):
+def whiten(pairs, block_row, traces, windows, inner, outer):
     channels = traces.shape[0]
-    share = channels // (far * near * SPLIT)
-    shape = (GROUPS, SPLIT, near, 2 * far * windows * share + NOTE, BINS)
+    share = channels // (inner * outer * SPLIT)
+    shape = (GROUPS, SPLIT, outer, 2 * inner * windows * share + NOTE, BINS)
     hbm = pl.BlockSpec(memory_space=pl.ANY)
     return pl.pallas_call(
-        functools.partial(whiten_kernel, windows, far, near),
+        functools.partial(whiten_kernel, windows, inner, outer),
         in_specs=[hbm, hbm, hbm, hbm],
         out_specs=pl.BlockSpec(memory_space=pltpu.VMEM),
         out_shape=pltpu.VMEM(shape, jnp.bfloat16),
@@ -132,15 +132,15 @@
 
 
 def cross_kernel(windows, spectra_ref, out_ref):
-    count, far, _, share, _ = out_ref.shape
-    near = spectra_ref.shape[1]
-    notes = [spectra_ref[i, 0, 2 * far * windows * share :].astype(jnp.float32) for i in range(count)]
+    count, inner, _, share, _ = out_ref.shape
+    outer = spectra_ref.shape[1]
+    notes = [spectra_ref[i, 0, 2 * inner * windows * share :].astype(jnp.float32) for i in range(count)]
     rows = [(note[0, 0].astype(jnp.int32), note[1, 0].astype(jnp.int32)) for note in notes]
     for i, (a, b) in enumerate(rows):
-        for f in range(far):
+        for f in range(inner):
             real = jnp.zeros(out_ref.shape[3:], jnp.float32)
             imag = jnp.zeros(out_ref.shape[3:], jnp.float32)
-            for n in range(near):
+            for n in range(outer):
                 for w in range(windows):
                     at = 2 * (f * windows + w) * share
                     re, im = slice(at, at + share), slice(at + share, at + 2 * share)
@@ -150,26 +150,26 @@
                     second_im = spectra_ref[b, n, im].astype(jnp.float32)
                     real += first_re * second_re + first_im * second_im
                     imag += first_re * second_im - first_im * second_re
-            out_ref[i, far - 1 - f, 0] = real.astype(jnp.bfloat16)
-            out_ref[i, far - 1 - f, 1] = imag.astype(jnp.bfloat16)
-
-
-def cross_groups(spectra, windows, far, share):
+            out_ref[i, inner - 1 - f, 0] = real.astype(jnp.bfloat16)
+            out_ref[i, inner - 1 - f, 1] = imag.astype(jnp.bfloat16)
+
+
+def cross_groups(spectra, windows, inner, share):
     vmem = pl.BlockSpec(memory_space=pltpu.VMEM)
     return pl.pallas_call(
         functools.partial(cross_kernel, windows),
         in_specs=[vmem],
         out_specs=vmem,
-        out_shape=jax.ShapeDtypeStruct((spectra.shape[0], far, 2, share, BINS), jnp.bfloat16),
+        out_shape=jax.ShapeDtypeStruct((spectra.shape[0], inner, 2, share, BINS), jnp.bfloat16),
         compiler_params=pltpu.CompilerParams(vmem_limit_bytes=8 * 2**20),
         name="cross",
     )(spectra)
 
 
-def cross_narrow(spectra, windows, far, share):
-    parts, near, rows, width = spectra.shape
+def cross_narrow(spectra, windows, inner, share):
+    parts, outer, rows, width = spectra.shape
     noted = spectra[:, 0, rows - NOTE : rows - NOTE + 2, 0].astype(jnp.int32)
-    parted = spectra[:, :, : rows - NOTE].reshape(parts, near, far, windows, 2, share, width)
+    parted = spectra[:, :, : rows - NOTE].reshape(parts, outer, inner, windows, 2, share, width)
     first = parted[noted[:, 0]].astype(jnp.float32)
     second = parted[noted[:, 1]].astype(jnp.float32)
     first_re, first_im, second_re, second_im = first[..., 0, :, :], first[..., 1, :, :], second[..., 0, :, :], second[..., 1, :, :]
@@ -180,18 +180,18 @@
 
 def inverse_kernel(cross_ref, table_ref, out_ref):
     depth = NB
-    far, share = cross_ref.shape[2], cross_ref.shape[4]
+    inner, share = cross_ref.shape[2], cross_ref.shape[4]
 
     def lags(parity):
         groups = range(parity * GROUPS // PARITIES, (parity + 1) * GROUPS // PARITIES)
         parts = [
             jnp.concatenate([cross_ref[g, h, f, part] for g in groups for part in range(2)], axis=1)
-            for f in range(far)
+            for f in range(inner)
             for h in range(SPLIT)
         ]
         table = table_ref[parity * depth : (parity + 1) * depth]
         product = jnp.dot(jnp.concatenate(parts, axis=0), table, preferred_element_type=jnp.float32)
-        return sum(product[f * SPLIT * share : (f + 1) * SPLIT * share] for f in range(far))
+        return sum(product[f * SPLIT * share : (f + 1) * SPLIT * share] for f in range(inner))
 
     a, b = lags(0), lags(1)
     out_ref[0, :, : LAGS // 2] = a + b
@@ -225,28 +225,28 @@
 def local(traces, pairs, block_row):
     _, channels, samples = traces.shape
     windows = samples // WIN
-    parts, far, near = lax.axis_size("pair"), lax.axis_size("far"), lax.axis_size("near")
+    parts, inner, outer = lax.axis_size("pair"), lax.axis_size("inner"), lax.axis_size("outer")
     per_group = parts // (GROUPS * SPLIT)
-    share = channels // (far * near * SPLIT)
+    share = channels // (inner * outer * SPLIT)
     width = BINS // per_group
-    rows = 2 * far * windows * share + NOTE
-    sent = whiten(pairs, block_row, traces[0], windows, far, near)
+    rows = 2 * inner * windows * share + NOTE
+    sent = whiten(pairs, block_row, traces[0], windows, inner, outer)
     if per_group > 1:
-        sent = sent.reshape(GROUPS, SPLIT, near, rows, per_group, width).transpose(0, 4, 1, 2, 3, 5)
+        sent = sent.reshape(GROUPS, SPLIT, outer, rows, per_group, width).transpose(0, 4, 1, 2, 3, 5)
     order = exchange_order(parts)
-    held = all_to_all(sent.reshape(parts * near, rows, width), order, "near")
+    held = all_to_all(sent.reshape(parts * outer, rows, width), order, "outer")
     cross_of = cross_groups if per_group == 1 else cross_narrow
-    cross = cross_of(held.reshape(parts, near, rows, width), windows, far, share)
-    mine = all_to_all(cross.reshape(parts * far, 2, share, width), order, "far")
-    mine = mine.reshape(GROUPS, per_group, SPLIT, far, 2, share, width)
-    mine = mine.transpose(0, 2, 3, 4, 5, 1, 6).reshape(GROUPS, SPLIT, far, 2, share, BINS)
-    return inverse(mine, 1.0 / (windows * far * near))
+    cross = cross_of(held.reshape(parts, outer, rows, width), windows, inner, share)
+    mine = all_to_all(cross.reshape(parts * inner, 2, share, width), order, "inner")
+    mine = mine.reshape(GROUPS, per_group, SPLIT, inner, 2, share, width)
+    mine = mine.transpose(0, 2, 3, 4, 5, 1, 6).reshape(GROUPS, SPLIT, inner, 2, share, BINS)
+    return inverse(mine, 1.0 / (windows * inner * outer))
 
 
 def solution(mesh):
     pairs, segs = mesh.devices.shape
-    split = jax.sharding.Mesh(mesh.devices.reshape(pairs, segs // NEAR, NEAR), ("pair", "far", "near"))
-    placed = (P("pair", None, ("far", "near")), P("pair", None), P())
+    split = jax.sharding.Mesh(mesh.devices.reshape(pairs, OUTER, segs // OUTER), ("pair", "outer", "inner"))
+    placed = (P("pair", None, ("outer", "inner")), P("pair", None), P())
     return jax.shard_map(
-        local, mesh=split, in_specs=placed, out_specs=P("pair", ("far", "near"), None), check_vma=False
+        local, mesh=split, in_specs=placed, out_specs=P("pair", ("outer", "inner"), None), check_vma=False
     )

time: 48.1 us -> 47.4 us (0.985)
  blocking collectives: 42.1 us -> 41.1 us
    all_to_all x2, blocking collectives: 42.1 us -> 41.1 us  [all_to_all(): lax.all_to_all(sent, ('pair', axis), split_axis=0, concat_axis=0, tiled=T...]
where the time goes in v7:
time: 47.4 us; the launch traced here: 47 us
  blocking collectives  41.1 us (87%)
  Pallas kernels  5.86 us (12%)
    all_to_all x2, blocking collectives, all_to_all(): lax.all_to_all(sent, ('pair', axis), split_axis=0, concat_axis=0, tiled=T...  41.1 us
    pallas_call x1, Pallas kernels, whiten(): pl.pallas_call(functools.partial(whiten_kernel, windows, inner, outer), i...  4.23 us
    pallas_call x1, Pallas kernels, inverse(): pl.pallas_call(inverse_kernel, in_specs=[vmem, vmem], out_specs=vmem, out...  1.19 us

profile of v7, /device:TPU:0, one launch (start us, length us, event | category | flops | bytes accessed | tf_op | source)
XLA Modules:
  0.0 47.0 jit_solution(2702767608190506478)
XLA Ops:
  0.0 4.2 %whiten.1 = bf16[4,2,2,264,128]{4,3,2,1,0:T(8,128)(2,1)S(1)} custom-call(s32[1,2]{1,0:T(1,128)} %pairs_hbm.1, s32[8]{0:T(128)} %row_hbm.1, bf16[128,8192]{1,0:T(8,128)(2,1)} %bitcast.9, bf16[2,1024,512]{2,1,0:T(8,128)(2,1)} %constant.4.clone.table_hbm), custom_call_target="tpu_custom_call" | custom-call | tf_op jit(solution)/shard_map/whiten/pallas_call | solution.py:115
  4.2 0.0 copy-start
  4.2 32.8 %all_to_all.10 = bf16[16,264,128]{2,1,0:T(8,128)(2,1)S(1)} all-to-all(bf16[16,264,128]{2,1,0:T(8,128)(2,1)S(1)} %bitcast.6), channel_id=1, replica_groups={{22,20,18,16,30,28,26,24,6,4,2,0,14,12,10,8},{23,21,19,17,31,29,27,25,7..., dimensions={0} | all-to-all | bytes 2162688 | tf_op jit(solution)/shard_map/all_to_all | solution.py:220
  37.0 0.4 cross.1
  37.5 8.3 %all_to_all.11 = bf16[16,2,16,128]{3,2,1,0:T(8,128)(2,1)S(1)} all-to-all(bf16[16,2,16,128]{3,2,1,0:T(8,128)(2,1)S(1)} %bitcast.8), channel_id=1, replica_groups={{21,20,17,16,29,28,25,24,5,4,1,0,13,12,9,8},{23,22,19,18,31,30,27,26,7,..., dimensions={0} | all-to-all | bytes 262144 | tf_op jit(solution)/shard_map/all_to_all | solution.py:220
  45.8 0.0 copy-done
  45.8 1.2 %inverse.1 = f32[1,32,2048]{2,1,0:T(8,128)} custom-call(bf16[4,2,2,2,16,128]{5,4,3,2,1,0:T(8,128)(2,1)S(1)} %bitcast.7, bf16[1024,1024]{1,0:T(8,128)(2,1)S(1)} %copy-done), custom_call_target="tpu_custom_call" | custom-call | tf_op jit(solution)/shard_map/inverse/pallas_call | solution.py:203
Async XLA Ops:
  4.2 41.5 %copy-start = (bf16[1024,1024]{1,0:T(8,128)(2,1)S(1)}, bf16[1024,1024]{1,0:T(8,128)(2,1)}, u32[]{:S(2)}) copy-start(bf16[1024,1024]{1,0:T(8,128)(2,1)} %constant.5.clone.table_ref) | copy-start | bytes 6291460

commit v8 on v7

--- a/solution.py
+++ b/solution.py
@@ -17,7 +17,7 @@
 GROUPS = NB // BINS
 SPLIT = 2
 PARITIES = 2
-NOTE = 8
+NOTE = 16
 OUTER = 2
 
 

time: 47.4 us -> 48 us (1.013)
  blocking collectives: 41.1 us -> 41.7 us
    all_to_all x2, blocking collectives: 41.1 us -> 41.7 us  [all_to_all(): lax.all_to_all(sent, ('pair', axis), split_axis=0, concat_axis=0, tiled=T...]
where the time goes in v8:
time: 48 us; the launch traced here: 47.6 us
  blocking collectives  41.7 us (87%)
  Pallas kernels  5.85 us (12%)
    all_to_all x2, blocking collectives, all_to_all(): lax.all_to_all(sent, ('pair', axis), split_axis=0, concat_axis=0, tiled=T...  41.7 us
    pallas_call x1, Pallas kernels, whiten(): pl.pallas_call(functools.partial(whiten_kernel, windows, inner, outer), i...  4.21 us
    pallas_call x1, Pallas kernels, inverse(): pl.pallas_call(inverse_kernel, in_specs=[vmem, vmem], out_specs=vmem, out...  1.19 us

profile of v8, /device:TPU:0, one launch (start us, length us, event | category | flops | bytes accessed | tf_op | source)
XLA Modules:
  0.0 47.6 jit_solution(4520037134566511107)
XLA Ops:
  0.0 4.2 %whiten.1 = bf16[4,2,2,272,128]{4,3,2,1,0:T(8,128)(2,1)S(1)} custom-call(s32[1,2]{1,0:T(1,128)} %pairs_hbm.1, s32[8]{0:T(128)} %row_hbm.1, bf16[128,8192]{1,0:T(8,128)(2,1)} %bitcast.9, bf16[2,1024,512]{2,1,0:T(8,128)(2,1)} %constant.4.clone.table_hbm), custom_call_target="tpu_custom_call" | custom-call | tf_op jit(solution)/shard_map/whiten/pallas_call | solution.py:115
  4.2 0.0 copy-start
  4.2 33.4 %all_to_all.10 = bf16[16,272,128]{2,1,0:T(8,128)(2,1)S(1)} all-to-all(bf16[16,272,128]{2,1,0:T(8,128)(2,1)S(1)} %bitcast.5), channel_id=1, replica_groups={{22,20,18,16,30,28,26,24,6,4,2,0,14,12,10,8},{23,21,19,17,31,29,27,25,7..., dimensions={0} | all-to-all | bytes 2228224 | tf_op jit(solution)/shard_map/all_to_all | solution.py:220
  37.7 0.4 cross.1
  38.1 8.3 %all_to_all.11 = bf16[16,2,16,128]{3,2,1,0:T(8,128)(2,1)S(1)} all-to-all(bf16[16,2,16,128]{3,2,1,0:T(8,128)(2,1)S(1)} %bitcast.8), channel_id=1, replica_groups={{21,20,17,16,29,28,25,24,5,4,1,0,13,12,9,8},{23,22,19,18,31,30,27,26,7,..., dimensions={0} | all-to-all | bytes 262144 | tf_op jit(solution)/shard_map/all_to_all | solution.py:220
  46.4 0.0 copy-done
  46.4 1.2 %inverse.1 = f32[1,32,2048]{2,1,0:T(8,128)} custom-call(bf16[4,2,2,2,16,128]{5,4,3,2,1,0:T(8,128)(2,1)S(1)} %bitcast.7, bf16[1024,1024]{1,0:T(8,128)(2,1)S(1)} %copy-done), custom_call_target="tpu_custom_call" | custom-call | tf_op jit(solution)/shard_map/inverse/pallas_call | solution.py:203
Async XLA Ops:
  4.2 42.2 %copy-start = (bf16[1024,1024]{1,0:T(8,128)(2,1)S(1)}, bf16[1024,1024]{1,0:T(8,128)(2,1)}, u32[]{:S(2)}) copy-start(bf16[1024,1024]{1,0:T(8,128)(2,1)} %constant.5.clone.table_ref) | copy-start | bytes 6291460

commit v9 on v7

--- a/solution.py
+++ b/solution.py
@@ -22,9 +22,7 @@
 
 
 def frequencies():
-    even = np.arange(2, NB + 1, 2)
-    odd = np.arange(1, NB + 1, 2)
-    return np.concatenate((even, odd)).reshape(GROUPS, BINS)
+    return np.stack([np.arange(first, NB + 1, 4) for first in (4, 2, 1, 3)])
 
 
 def forward_table():
@@ -34,10 +32,10 @@
 
 
 def inverse_table(scale):
-    shifts = np.arange(LAGS // 2) - LAGS // 2
+    shifts = np.arange(LAGS // 4) - LAGS // 2
     phase = (frequencies()[:, :, None] * shifts % WIN) * (2.0 * np.pi / WIN)
     table = np.stack((np.cos(phase), -np.sin(phase)), axis=1) * scale
-    return table.reshape(2 * NB, LAGS // 2).astype(ml_dtypes.bfloat16)
+    return table.reshape(2 * NB, LAGS // 4).astype(ml_dtypes.bfloat16)
 
 
 def whiten_kernel(windows, inner, outer, pairs_hbm, row_hbm, traces_hbm, table_hbm, sent, pairs_ref, row_ref, frames, table, small_sem, frame_sem, table_sem):
@@ -179,23 +177,32 @@
 
 
 def inverse_kernel(cross_ref, table_ref, out_ref):
-    depth = NB
     inner, share = cross_ref.shape[2], cross_ref.shape[4]
+    rows, quarter = SPLIT * share, LAGS // 4
 
     def lags(parity):
-        groups = range(parity * GROUPS // PARITIES, (parity + 1) * GROUPS // PARITIES)
-        parts = [
-            jnp.concatenate([cross_ref[g, h, f, part] for g in groups for part in range(2)], axis=1)
-            for f in range(inner)
-            for h in range(SPLIT)
+        parts = []
+        for turned in range(2):
+            for f in range(inner):
+                for h in range(SPLIT):
+                    (re0, im0), (re1, im1) = (
+                        (cross_ref[g, h, f, 0], cross_ref[g, h, f, 1]) for g in (2 * parity, 2 * parity + 1)
+                    )
+                    if turned and parity == 0:
+                        re1, im1 = -re1, -im1
+                    elif turned:
+                        re0, im0, re1, im1 = -im0, re0, im1, -re1
+                    parts.append(jnp.concatenate((re0, im0, re1, im1), axis=1))
+        table = table_ref[parity * NB : (parity + 1) * NB]
+        product = jnp.dot(jnp.concatenate(parts, axis=0), table, preferred_element_type=jnp.float32)
+        return [
+            sum(product[(q * inner + f) * rows : (q * inner + f + 1) * rows] for f in range(inner)) for q in range(2)
         ]
-        table = table_ref[parity * depth : (parity + 1) * depth]
-        product = jnp.dot(jnp.concatenate(parts, axis=0), table, preferred_element_type=jnp.float32)
-        return sum(product[f * SPLIT * share : (f + 1) * SPLIT * share] for f in range(inner))
-
-    a, b = lags(0), lags(1)
-    out_ref[0, :, : LAGS // 2] = a + b
-    out_ref[0, :, LAGS // 2 :] = a - b
+
+    even, odd = lags(0), lags(1)
+    for q in range(4):
+        a, b = even[q % 2], odd[q % 2]
+        out_ref[0, :, q * quarter : (q + 1) * quarter] = a + b if q < 2 else a - b
 
 
 def inverse(cross, scale):

time: 47.4 us -> 47.2 us (level)
  no operation moved by 1% of the time
where the time goes in v9:
time: 47.2 us; the launch traced here: 46.8 us
  blocking collectives  41.1 us (87%)
  Pallas kernels  5.7 us (12%)
    all_to_all x2, blocking collectives, all_to_all(): lax.all_to_all(sent, ('pair', axis), split_axis=0, concat_axis=0, tiled=T...  41.1 us
    pallas_call x1, Pallas kernels, whiten(): pl.pallas_call(functools.partial(whiten_kernel, windows, inner, outer), i...  4.23 us
    pallas_call x1, Pallas kernels, inverse(): pl.pallas_call(inverse_kernel, in_specs=[vmem, vmem], out_specs=vmem, out...  1.02 us

profile of v9, /device:TPU:0, one launch (start us, length us, event | category | flops | bytes accessed | tf_op | source)
XLA Modules:
  0.0 46.8 jit_solution(11186465072988569706)
XLA Ops:
  0.0 4.2 %whiten.1 = bf16[4,2,2,264,128]{4,3,2,1,0:T(8,128)(2,1)S(1)} custom-call(s32[1,2]{1,0:T(1,128)} %pairs_hbm.1, s32[8]{0:T(128)} %row_hbm.1, bf16[128,8192]{1,0:T(8,128)(2,1)} %bitcast.9, bf16[2,1024,512]{2,1,0:T(8,128)(2,1)} %constant.4.clone.table_hbm), custom_call_target="tpu_custom_call" | custom-call | tf_op jit(solution)/shard_map/whiten/pallas_call | solution.py:113
  4.2 0.0 copy-start
  4.2 32.8 %all_to_all.10 = bf16[16,264,128]{2,1,0:T(8,128)(2,1)S(1)} all-to-all(bf16[16,264,128]{2,1,0:T(8,128)(2,1)S(1)} %bitcast.6), channel_id=1, replica_groups={{22,20,18,16,30,28,26,24,6,4,2,0,14,12,10,8},{23,21,19,17,31,29,27,25,7..., dimensions={0} | all-to-all | bytes 2162688 | tf_op jit(solution)/shard_map/all_to_all | solution.py:227
  37.0 0.4 cross.1
  37.5 8.3 %all_to_all.11 = bf16[16,2,16,128]{3,2,1,0:T(8,128)(2,1)S(1)} all-to-all(bf16[16,2,16,128]{3,2,1,0:T(8,128)(2,1)S(1)} %bitcast.7), channel_id=1, replica_groups={{21,20,17,16,29,28,25,24,5,4,1,0,13,12,9,8},{23,22,19,18,31,30,27,26,7,..., dimensions={0} | all-to-all | bytes 262144 | tf_op jit(solution)/shard_map/all_to_all | solution.py:227
  45.8 0.0 copy-done
  45.8 1.0 %inverse.1 = f32[1,32,2048]{2,1,0:T(8,128)} custom-call(bf16[4,2,2,2,16,128]{5,4,3,2,1,0:T(8,128)(2,1)S(1)} %bitcast.8, bf16[1024,512]{1,0:T(8,128)(2,1)S(1)} %copy-done), custom_call_target="tpu_custom_call" | custom-call | tf_op jit(solution)/shard_map/inverse/pallas_call | solution.py:210
Async XLA Ops:
  4.2 41.5 %copy-start = (bf16[1024,512]{1,0:T(8,128)(2,1)S(1)}, bf16[1024,512]{1,0:T(8,128)(2,1)}, u32[]{:S(2)}) copy-start(bf16[1024,512]{1,0:T(8,128)(2,1)} %constant.5.clone.table_ref) | copy-start | bytes 3145732
